TPU v7x, 256 devices: a whole 4x4x8 slice. The times are simulated.
256 devices in a mesh: pos: 32 (over x, z), grp: 8 (over y, core).
Axes of the slice: x: 4, y: 4, z: 8, core: 2. Of those that a mesh axis runs over, the one named last changes fastest.
Arguments:
- key_cache: bfloat16 [262144, 2048], P(('grp', 'pos')), parts along dimension 0, may hold values from -60 to 60
- init_basis: float32 [16384, 256], P('grp'), parts along dimension 0, may hold values from -0.125 to 0.125
Outputs:
- basis_scaled: float32 [16384, 256], P('grp'), parts along dimension 0
- latents: bfloat16 [262144, 256], P(('grp', 'pos')), parts along dimension 0
There are 8 independent parts, one for each index of `grp`. A program takes and returns all parts, laid end to end along the dimension named above; each array names one. Nothing has to cross between parts.
All inputs are finite; a program needn't handle non-finite values.
Results may differ from a plain program's by a relative error of at most 0.0095.
Values may be sent and summed in bfloat16 or wider, within the bound.
No kernel may reach another device: no remote copies, remote signals or barrier semaphores. Data moves between devices by JAX's collectives and lax.ppermute only.
A program may use at most 64 MiB of HBM per device.

v0:
```python
import jax
import jax.numpy as jnp
from jax import lax
from jax.sharding import PartitionSpec as P

ITERS = 3


def solve_rows(factor, summed):
    return jax.scipy.linalg.solve_triangular(factor, summed.T, lower=True).T


def local(key_cache, init_basis):
    feature_width = key_cache.shape[1]
    basis = init_basis
    rounded = init_basis.astype(jnp.bfloat16)
    for sweep in range(ITERS):
        projected = jnp.dot(key_cache, rounded, preferred_element_type=jnp.float32).astype(
            jnp.bfloat16
        )
        local_term = lax.dot_general(
            key_cache, projected, (((0,), (0,)), ((), ())), preferred_element_type=jnp.float32
        )
        summed = lax.psum(local_term, "pos")
        gram_matrix = jnp.dot(summed.T, summed, precision=lax.Precision.HIGHEST)
        factor = jnp.linalg.cholesky(gram_matrix)
        basis = solve_rows(factor, summed)
        rounded = basis.astype(jnp.bfloat16)
    compressed = jnp.dot(
        key_cache, basis.astype(jnp.bfloat16), preferred_element_type=jnp.float32
    ).astype(jnp.bfloat16)
    latents = lax.all_to_all(compressed, "pos", split_axis=0, concat_axis=0, tiled=True)
    return (jnp.sqrt(jnp.float32(feature_width)) * basis, latents)


def solution(mesh):
    placed = (P(("grp", "pos"), None), P("grp", None))
    return jax.shard_map(
        local,
        mesh=mesh,
        in_specs=placed,
        out_specs=(P("grp", None), P(("grp", "pos"), None)),
        check_vma=False,
    )
```

profile of v0, /device:TPU:56, one launch (start us, length us, event | category | flops | bytes accessed | tf_op | source)
XLA Modules:
  0.0 725.4 jit_solution(11845498469614559256)
XLA Ops:
  7.2 9.8 %convolution_bitcast_fusion.2 = f32[2048,256]{0,1:T(8,128)} fusion(bf16[1024,2048]{1,0:T(8,128)(2,1)} %param.5, f32[2048,256]{1,0:T(8,128)} %param.6), kind=kOutput, calls=%fused_computation.8 | convolution fusion | flops 2148270080 | bytes 8388608 | tf_op jit(solution)/shard_map/dot_general | solution.py:21
  17.3 155.0 %all-reduce.5.cloned.1.call-done = f32[2048,256]{0,1:T(8,128)} async-done(((f32[2048,256]{0,1:T(8,128)}), f32[2048,256]{0,1:T(8,128)}) %all-reduce.5.cloned.1.call-update) | async-done | bytes 2097168 | tf_op jit(solution)/shard_map/psum | solution.py:24
  172.3 4.1 fusion.46
  176.6 11.7 %cholesky.172 = f32[128,128]{1,0:T(8,128)S(1)} custom-call(f32[128,128]{1,0:T(8,128)S(1)} %cholesky.270), custom_call_target="Cholesky" | custom-call | tf_op jit(solution)/shard_map/jit(cholesky)/cholesky | solution.py:26
  188.3 9.8 %custom-call.15 = f32[1,128,128]{1,2,0:T(8,128)S(1)} custom-call(f32[1,128,128]{2,1,0:T(8,128)S(1)} %get-tuple-element.72), custom_call_target="InvertDiagBlocksLowerTriangular" | custom-call | tf_op jit(solution)/shard_map/jit(cholesky)/cholesky | solution.py:26
  198.6 11.9 %cholesky.189 = f32[128,128]{1,0:T(8,128)S(1)} custom-call(f32[128,128]{1,0:T(8,128)S(1)} %convolution_subtract_fusion.5), custom_call_target="Cholesky" | custom-call | tf_op jit(solution)/shard_map/jit(cholesky)/cholesky | solution.py:26
  212.6 3.9 while.6
  213.3 1.3 bitcast_dynamic-update-slice_fusion.6
  216.6 19.7 %custom-call.16 = f32[2,128,128]{1,2,0:T(8,128)S(1)} custom-call(f32[2,128,128]{2,1,0:T(8,128)S(1)} %get-tuple-element.24), custom_call_target="InvertDiagBlocksLowerTriangular" | custom-call | tf_op jit(solution)/shard_map/jit(_solve_triangular)/triangular_solve | solution.py:10
  239.4 7.2 convolution_bitcast_fusion.1
  247.0 151.0 %all-reduce.7.cloned.1.call-done = f32[2048,256]{0,1:T(8,128)} async-done(((f32[2048,256]{0,1:T(8,128)}), f32[2048,256]{0,1:T(8,128)}) %all-reduce.7.cloned.1.call-update) | async-done | bytes 2097168 | tf_op jit(solution)/shard_map/psum | solution.py:24
  398.0 4.1 fusion.47
  402.3 11.7 %cholesky.206 = f32[128,128]{1,0:T(8,128)S(1)} custom-call(f32[128,128]{1,0:T(8,128)S(1)} %cholesky.273), custom_call_target="Cholesky" | custom-call | tf_op jit(solution)/shard_map/jit(cholesky)/cholesky | solution.py:26
  414.1 9.8 %custom-call.17 = f32[1,128,128]{1,2,0:T(8,128)S(1)} custom-call(f32[1,128,128]{2,1,0:T(8,128)S(1)} %get-tuple-element.68), custom_call_target="InvertDiagBlocksLowerTriangular" | custom-call | tf_op jit(solution)/shard_map/jit(cholesky)/cholesky | solution.py:26
  424.4 11.9 %cholesky.223 = f32[128,128]{1,0:T(8,128)S(1)} custom-call(f32[128,128]{1,0:T(8,128)S(1)} %convolution_subtract_fusion.4), custom_call_target="Cholesky" | custom-call | tf_op jit(solution)/shard_map/jit(cholesky)/cholesky | solution.py:26
  438.9 3.9 while.7
  442.8 19.7 %custom-call.18 = f32[2,128,128]{1,2,0:T(8,128)S(1)} custom-call(f32[2,128,128]{2,1,0:T(8,128)S(1)} %get-tuple-element.25), custom_call_target="InvertDiagBlocksLowerTriangular" | custom-call | tf_op jit(solution)/shard_map/jit(_solve_triangular)/triangular_solve | solution.py:10
  465.6 7.2 convolution_bitcast_fusion
  472.8 151.4 %all-reduce.9.cloned.1.call-done = f32[2048,256]{0,1:T(8,128)} async-done(((f32[2048,256]{0,1:T(8,128)}), f32[2048,256]{0,1:T(8,128)}) %all-reduce.9.cloned.1.call-update) | async-done | bytes 2097168 | tf_op jit(solution)/shard_map/psum | solution.py:24
  624.2 4.1 fusion.48
  628.5 11.7 %cholesky.240 = f32[128,128]{1,0:T(8,128)S(1)} custom-call(f32[128,128]{1,0:T(8,128)S(1)} %cholesky.276), custom_call_target="Cholesky" | custom-call | tf_op jit(solution)/shard_map/jit(cholesky)/cholesky | solution.py:26
  640.3 10.0 %custom-call.19 = f32[1,128,128]{1,2,0:T(8,128)S(1)} custom-call(f32[1,128,128]{2,1,0:T(8,128)S(1)} %get-tuple-element.64), custom_call_target="InvertDiagBlocksLowerTriangular" | custom-call | tf_op jit(solution)/shard_map/jit(cholesky)/cholesky | solution.py:26
  650.8 11.7 %cholesky.257 = f32[128,128]{1,0:T(8,128)S(1)} custom-call(f32[128,128]{1,0:T(8,128)S(1)} %convolution_subtract_fusion.3), custom_call_target="Cholesky" | custom-call | tf_op jit(solution)/shard_map/jit(cholesky)/cholesky | solution.py:26
  665.1 3.9 while.8
  665.8 1.4 bitcast_dynamic-update-slice_fusion.8
  667.7 1.4 bitcast_dynamic-update-slice_fusion.8
  669.1 19.7 %custom-call.20 = f32[2,128,128]{1,2,0:T(8,128)S(1)} custom-call(f32[2,128,128]{2,1,0:T(8,128)S(1)} %get-tuple-element.26), custom_call_target="InvertDiagBlocksLowerTriangular" | custom-call | tf_op jit(solution)/shard_map/jit(_solve_triangular)/triangular_solve | solution.py:10
  695.2 7.3 %all-to-all-start = ((bf16[32,32,256]{2,1,0:T(8,128)(2,1)}), bf16[32,32,256]{2,1,0:T(8,128)(2,1)}, u32[]{:S(2)}, u32[]{:S(2)}) async-start(bf16[32,32,256]{2,1,0:T(8,128)(2,1)} %bitcast.23), calls=%async_computation | async-start | bytes 1048576 | tf_op jit(solution)/shard_map/all_to_all | solution.py:32
  702.5 1.4 multiply_bitcast_fusion
  704.0 1.8 copy.13
  705.8 11.0 %all-to-all-done = bf16[32,32,256]{2,1,0:T(8,128)(2,1)} async-done(((bf16[32,32,256]{2,1,0:T(8,128)(2,1)}), bf16[32,32,256]{2,1,0:T(8,128)(2,1)}, u32[]{:S(2)}, u32[]{:S(2)}) %all-to-all-start) | async-done | bytes 524320 | tf_op jit(solution)/shard_map/all_to_all | solution.py:32
  716.8 1.9 copy.50
  (79 shorter events, 26.6 us)
Async XLA Ops:
  7.2 165.1 %all-reduce.5.cloned.1.call-start = ((), (), s32[]{:S(2)}) async-start(), calls=%async_computation.1 | async-start | bytes 4194304 | tf_op jit(solution)/shard_map/psum | solution.py:24
  17.0 380.9 %all-reduce.7.cloned.1.call-start = ((), (), s32[]{:S(2)}) async-start(), calls=%async_computation.2 | async-start | bytes 4194304 | tf_op jit(solution)/shard_map/psum | solution.py:24
  176.4 59.9 %copy-start = (f32[2048,256]{0,1:T(8,128)S(1)}, f32[2048,256]{0,1:T(8,128)}, u32[]{:S(2)}) copy-start(f32[2048,256]{0,1:T(8,128)} %all-reduce.5.cloned.1.call-done) | copy-start | bytes 6291460
  246.6 377.6 %all-reduce.9.cloned.1.call-start = ((), (), s32[]{:S(2)}) async-start(), calls=%async_computation.3 | async-start | bytes 4194304 | tf_op jit(solution)/shard_map/psum | solution.py:24
  402.1 60.4 %copy-start.1 = (f32[2048,256]{0,1:T(8,128)S(1)}, f32[2048,256]{0,1:T(8,128)}, u32[]{:S(2)}) copy-start(f32[2048,256]{0,1:T(8,128)} %all-reduce.7.cloned.1.call-done) | copy-start | bytes 6291460
  628.3 60.5 %copy-start.2 = (f32[2048,256]{0,1:T(8,128)S(1)}, f32[2048,256]{0,1:T(8,128)}, u32[]{:S(2)}) copy-start(f32[2048,256]{0,1:T(8,128)} %all-reduce.9.cloned.1.call-done) | copy-start | bytes 6291460
  689.8 3.1 copy-start.4
  691.9 1.0 copy-start.3
  695.2 21.6 %all-to-all-start = ((bf16[32,32,256]{2,1,0:T(8,128)(2,1)}), bf16[32,32,256]{2,1,0:T(8,128)(2,1)}, u32[]{:S(2)}, u32[]{:S(2)}) async-start(bf16[32,32,256]{2,1,0:T(8,128)(2,1)} %bitcast.23), calls=%async_computation | async-start | bytes 1048576 | tf_op jit(solution)/shard_map/all_to_all | solution.py:32
Sparse Core Ops, SparseCore 0:
  17.2 155.0 all-reduce.4
  246.7 151.2 all-reduce.6
  472.9 151.2 all-reduce.8
where the time goes:
time: 730 us; the launch traced here: 725 us
  waiting for transfers between devices  468 us (64%)
  other arithmetic  164 us (22%)
  matrix products  48.4 us (7%)
  between operations  18.2 us (2%)
  local copies, waits for them, and re-layouts  17.9 us (2%)
  starting transfers between devices  8.03 us (1%)
    psum x3, waiting for transfers between devices, local(): summed = lax.psum(local_term, 'pos')  457 us
    another operation x20, other arithmetic, local(): factor = jnp.linalg.cholesky(gram_matrix)  104 us
    another operation x7, other arithmetic, solve_rows(): return jax.scipy.linalg.solve_triangular(factor, summed.T, lower=True).T  59.1 us
    dot_general x3, matrix products, local(): lax.dot_general(key_cache, projected, (((0,), (0,)), ((), ())), preferred...  24.1 us
  transfers between devices with their start and end apart: 4, of which 4 were waited for; matrix products, arithmetic and copies ran while one was open for 0% of the time, Pallas kernels for 0%

commit v1 on v0

v1 whole, which is shorter than its diff:
```python
import functools

import jax
import jax.numpy as jnp
from jax import lax
from jax.experimental import pallas as pl
from jax.experimental.pallas import tpu as pltpu
from jax.sharding import Mesh
from jax.sharding import PartitionSpec as P

ITERS = 3
NX = 4
NZ = 8
NB = 32
VMEM_BYTES = 40 * 1024 * 1024
F32 = jnp.float32
BF16 = jnp.bfloat16

NN = (((1,), (0,)), ((), ()))
NT = (((1,), (1,)), ((), ()))
TN = (((0,), (0,)), ((), ()))


def dot(a, b, dims):
    return lax.dot_general(a, b, dims, preferred_element_type=F32)


def exact_dot(a, b, dims):
    return lax.dot_general(a, b, dims, precision=lax.Precision.HIGHEST, preferred_element_type=F32)


def eliminate(rows, inverse, block):
    n = rows.shape[1]
    row_id = lax.broadcasted_iota(jnp.int32, (NB, 1), 0)
    pivots = jnp.ones((NB, 1), F32)
    for strip in range(NB // 8):
        first = block * NB + strip * 8
        columns = [rows[:, first + s : first + s + 1] for s in range(8)]
        columns = [jnp.broadcast_to(c, (NB, 128)) for c in columns]
        for s in range(8):
            k = strip * 8 + s
            pivot = columns[s][k : k + 1, :]
            below = jnp.where(row_id > k, columns[s] * (1.0 / pivot), 0.0)
            pivots = jnp.where(row_id == k, pivot, pivots)
            for later in range(s + 1, 8):
                columns[later] = columns[later] - below * columns[later][k : k + 1, :]
            wide = jnp.concatenate([below] * (n // 128), axis=1)
            rows = rows - wide * rows[k : k + 1, :]
            inverse = inverse - wide * inverse[k : k + 1, :]
    scale = lax.rsqrt(pivots)
    scale = jnp.concatenate([scale] * (n // 128), axis=1)
    return rows * scale, inverse * scale


def inverse_factor(gram, inv):
    n = gram.shape[0]
    eye = lax.broadcasted_iota(jnp.int32, (n, n), 0) == lax.broadcasted_iota(jnp.int32, (n, n), 1)
    inv[...] = eye.astype(F32)
    for block in range(n // NB):
        here = pl.ds(block * NB, NB)
        upper, lower = eliminate(gram[here, :], inv[here, :], block)
        inv[here, :] = lower
        done = (block + 1) * NB
        if done < n:
            factor = upper.T[done:, :]
            rest = pl.ds(done, n - done)
            gram[rest, :] = gram[rest, :] - exact_dot(factor, upper, NN)
            inv[rest, :] = inv[rest, :] - exact_dot(factor, lower, NN)


def split(a):
    high = a.astype(BF16)
    rest = a - high.astype(F32)
    mid = rest.astype(BF16)
    low = (rest - mid.astype(F32)).astype(BF16)
    return high, mid, low


def products(keys, basis, out):
    width = basis[0].shape[1]
    projected = 0.0
    for x in range(NX):
        projected = projected + dot(basis[x], keys[:, x * width : (x + 1) * width], NT)
    projected = projected.astype(BF16)
    for x in range(NX):
        out[x] = dot(projected, keys[:, x * width : (x + 1) * width], NN).astype(BF16)


def first_kernel(keys, basis, out):
    products(keys, [basis[x] for x in range(NX)], out)


def factor_of(summed, gram, inv):
    total = 0.0
    for x in range(NX):
        total = total + dot(summed[x], summed[x], NT)
    gram[...] = total
    inverse_factor(gram, inv)
    return split(inv[...])


def middle_kernel(summed, keys_hbm, out, gram, inv, keys, sem):
    copy = pltpu.make_async_copy(keys_hbm, keys, sem)
    copy.start()
    parts = factor_of(summed, gram, inv)
    basis = [sum(dot(p, summed[x], NN) for p in parts).astype(BF16) for x in range(NX)]
    copy.wait()
    products(keys, basis, out)


def last_kernel(summed, keys_hbm, basis_out, out, gram, inv, keys, sem):
    copy = pltpu.make_async_copy(keys_hbm, keys, sem)
    copy.start()
    parts = factor_of(summed, gram, inv)
    width = summed.shape[2]
    scale = jnp.sqrt(F32(NX * width))
    basis = [sum(dot(p, summed[x], NN) for p in parts) for x in range(NX)]
    for x in range(NX):
        basis_out[pl.ds(x * width, width), :] = (basis[x] * scale).T
    copy.wait()
    compressed = 0.0
    for x in range(NX):
        compressed = compressed + dot(keys[:, x * width : (x + 1) * width], basis[x].astype(BF16), NT)
    out[...] = compressed.astype(BF16)


def call(body, out_shape, operands, in_hbm, scratch):
    spec = [pl.BlockSpec(memory_space=pl.ANY if h else pltpu.VMEM) for h in in_hbm]
    return pl.pallas_call(
        body,
        out_shape=out_shape,
        in_specs=spec,
        out_specs=jax.tree.map(lambda _: pl.BlockSpec(memory_space=pltpu.VMEM), out_shape),
        scratch_shapes=scratch,
        compiler_params=pltpu.CompilerParams(vmem_limit_bytes=VMEM_BYTES),
    )(*operands)


def sum_and_spread(local_term):
    _, rank, width = local_term.shape
    part = rank // NZ
    terms = lax.all_to_all(local_term, "x", 0, 0, tiled=True)
    total = jnp.sum(terms.astype(F32), axis=0).astype(BF16).reshape(NZ, part, width)
    terms = lax.all_to_all(total, "z", 0, 0, tiled=True)
    total = jnp.sum(terms.astype(F32), axis=0).astype(BF16)
    total = jnp.broadcast_to(total[None], (NZ, part, width))
    block = lax.all_to_all(total, "z", 0, 0, tiled=True).reshape(1, rank, width)
    return lax.all_to_all(jnp.broadcast_to(block, (NX, rank, width)), "x", 0, 0, tiled=True)


def local(key_cache, init_basis):
    positions, features = key_cache.shape
    rank = init_basis.shape[1]
    width = features // NX
    shape = jax.ShapeDtypeStruct
    scratch = [
        pltpu.VMEM((rank, rank), F32),
        pltpu.VMEM((rank, rank), F32),
        pltpu.VMEM((positions, features), BF16),
        pltpu.SemaphoreType.DMA,
    ]
    blocks = shape((NX, rank, width), BF16)
    rounded = init_basis.astype(BF16).reshape(NX, width, rank).transpose(0, 2, 1)
    term = call(first_kernel, blocks, (key_cache, rounded), (False, False), [])
    for sweep in range(ITERS - 1):
        summed = sum_and_spread(term)
        term = call(middle_kernel, blocks, (summed, key_cache), (False, True), scratch)
    summed = sum_and_spread(term)
    outs = (shape((features, rank), F32), shape((positions, rank), BF16))
    basis, compressed = call(last_kernel, outs, (summed, key_cache), (False, True), scratch)
    latents = lax.all_to_all(compressed, ("x", "z"), split_axis=0, concat_axis=0, tiled=True)
    return basis, latents


def solution(mesh):
    grid = Mesh(mesh.devices.reshape(NX, NZ, -1), ("x", "z", "grp"))
    return jax.shard_map(
        local,
        mesh=grid,
        in_specs=(P(("grp", "x", "z"), None), P("grp", None)),
        out_specs=(P("grp", None), P(("grp", "x", "z"), None)),
        check_vma=False,
    )
```

time: 730 us -> 238 us (0.33)
  waiting for transfers between devices: 468 us -> 0 us
  blocking collectives: 0 us -> 190 us
  other arithmetic: 164 us -> 2.54 us
  matrix products: 48.4 us -> 0 us
  Pallas kernels: 0 us -> 40.9 us
  between operations: 18.2 us -> 0.77 us
  local copies, waits for them, and re-layouts: 17.9 us -> 3.82 us
  starting transfers between devices: 8.03 us -> 0 us
    psum x3 -> x0, waiting for transfers between devices: 457 us -> none  [local(): summed = lax.psum(local_term, 'pos')]
    all_to_all x0 -> x13, blocking collectives: none -> 190 us  [the longest x3 46.2 us: sum_and_spread(): terms = lax.all_to_all(total, 'z', 0, 0, tiled=True)]
    another operation x27 -> x0, other arithmetic: 163 us -> none  [the longest x20 104 us: local(): factor = jnp.linalg.cholesky(gram_matrix)]
    pallas_call x0 -> x4, Pallas kernels: none -> 40.9 us  [call(): pl.pallas_call(body, out_shape=out_shape, in_specs=spec, out_specs=jax.tr...]
    dot_general x7 -> x0, matrix products: 37.6 us -> none  [the longest x3 24.1 us: local(): lax.dot_general(key_cache, projected, (((0,), (0,)), ((), ())), preferred...]
    another operation x28 -> x0, local copies, waits for them, and re-layouts: 11.8 us -> none  [the longest x22 11.7 us: solve_rows(): return jax.scipy.linalg.solve_triangular(factor, summed.T, lower=True).T]
    all_to_all x1 -> x0, waiting for transfers between devices: 11 us -> none  [local(): lax.all_to_all(compressed, 'pos', split_axis=0, concat_axis=0, tiled=True)]
    another operation x15 -> x0, matrix products: 10.8 us -> none  [the longest x9 9.34 us: solve_rows(): return jax.scipy.linalg.solve_triangular(factor, summed.T, lower=True).T]
  transfers between devices with their start and end apart: 4 -> 0, of which waited for: 4 -> 0; matrix products, arithmetic and copies ran while one was open for 0% -> 0% of each run, Pallas kernels for 0% -> 0%
where the time goes in v1:
time: 238 us
  blocking collectives  190 us (80%)
  Pallas kernels  40.9 us (17%)
  local copies, waits for them, and re-layouts  3.82 us (2%)
  other arithmetic  2.54 us (1%)
    all_to_all x3, blocking collectives, sum_and_spread(): terms = lax.all_to_all(total, 'z', 0, 0, tiled=True)  46.2 us
    all_to_all x3, blocking collectives, sum_and_spread(): terms = lax.all_to_all(local_term, 'x', 0, 0, tiled=True)  45.8 us
    pallas_call x4, Pallas kernels, call(): pl.pallas_call(body, out_shape=out_shape, in_specs=spec, out_specs=jax.tr...  40.9 us
    all_to_all x3, blocking collectives, sum_and_spread(): lax.all_to_all(jnp.broadcast_to(block, (NX, rank, width)), 'x', 0, 0, til...  40.8 us
    all_to_all x3, blocking collectives, sum_and_spread(): block = lax.all_to_all(total, 'z', 0, 0, tiled=True).reshape(1, rank, width)  39.5 us
    all_to_all x1, blocking collectives, local(): lax.all_to_all(compressed, ('x', 'z'), split_axis=0, concat_axis=0, tiled...  17.6 us

profile of v1, /device:TPU:56, one launch (start us, length us, event | category | flops | bytes accessed | tf_op | source)
XLA Modules:
  0.0 237.9 jit_solution(8565656574203132889)
XLA Ops:
  0.6 1.7 convert_element_type.2
  2.3 0.5 copy.5
  2.9 0.0 copy-start
  2.9 2.2 copy-done
  5.1 2.4 shard_map.41
  7.4 19.2 %all_to_all.72 = bf16[4,256,512]{2,1,0:T(8,128)(2,1)S(1)} all-to-all(bf16[4,256,512]{2,1,0:T(8,128)(2,1)S(1)} %shard_map.41), channel_id=1, replica_groups=mesh['x'=4,'z'=8,'grp'=8] {'x'}, dimensions={0} | all-to-all | bytes 2097152 | tf_op jit(solution)/shard_map/all_to_all | solution.py:142
  26.6 0.2 reduce_sum.72
  26.9 17.6 %all_to_all.73 = bf16[8,32,512]{2,1,0:T(8,128)(2,1)S(1)} all-to-all(bf16[8,32,512]{2,1,0:T(8,128)(2,1)S(1)} %bitcast.14), channel_id=1, replica_groups=mesh['x'=4,'z'=8,'grp'=8] {'z'}, dimensions={0} | all-to-all | bytes 524288 | tf_op jit(solution)/shard_map/all_to_all | solution.py:144
  44.5 0.0 copy-start.1
  44.6 12.8 %all_to_all.74 = bf16[8,32,512]{2,1,0:T(8,128)(2,1)S(1)} all-to-all(bf16[8,32,512]{2,1,0:T(8,128)(2,1)S(1)} %broadcast_in_dim.18), channel_id=1, replica_groups=mesh['x'=4,'z'=8,'grp'=8] {'z'}, dimensions={0} | all-to-all | bytes 524288 | tf_op jit(solution)/shard_map/all_to_all | solution.py:147
  57.4 0.1 broadcast_in_dim.20
  57.5 14.1 %all_to_all.75.summed = bf16[4,256,512]{2,1,0:T(8,128)(2,1)S(1)} all-to-all(bf16[4,256,512]{2,1,0:T(8,128)(2,1)S(1)} %broadcast_in_dim.20), channel_id=1, replica_groups=mesh['x'=4,'z'=8,'grp'=8] {'x'}, dimensions={0} | all-to-all | bytes 2097152 | tf_op jit(solution)/shard_map/all_to_all | solution.py:148
  71.6 0.0 copy-done.1
  71.6 13.2 %shard_map.42 = bf16[4,256,512]{2,1,0:T(8,128)(2,1)S(1)} custom-call(bf16[4,256,512]{2,1,0:T(8,128)(2,1)S(1)} %all_to_all.75.summed, bf16[1024,2048]{1,0:T(8,128)(2,1)S(1)} %copy-done.1), custom_call_target="tpu_custom_call" | custom-call | tf_op jit(solution)/shard_map/pallas_call | solution.py:129
  84.8 13.3 %all_to_all.76 = bf16[4,256,512]{2,1,0:T(8,128)(2,1)S(1)} all-to-all(bf16[4,256,512]{2,1,0:T(8,128)(2,1)S(1)} %shard_map.42), channel_id=1, replica_groups=mesh['x'=4,'z'=8,'grp'=8] {'x'}, dimensions={0} | all-to-all | bytes 2097152 | tf_op jit(solution)/shard_map/all_to_all | solution.py:142
  98.1 0.2 reduce_sum.74
  98.3 13.2 %all_to_all.77 = bf16[8,32,512]{2,1,0:T(8,128)(2,1)S(1)} all-to-all(bf16[8,32,512]{2,1,0:T(8,128)(2,1)S(1)} %bitcast.16), channel_id=1, replica_groups=mesh['x'=4,'z'=8,'grp'=8] {'z'}, dimensions={0} | all-to-all | bytes 524288 | tf_op jit(solution)/shard_map/all_to_all | solution.py:144
  111.5 0.0 copy-start.2
  111.6 13.2 %all_to_all.78 = bf16[8,32,512]{2,1,0:T(8,128)(2,1)S(1)} all-to-all(bf16[8,32,512]{2,1,0:T(8,128)(2,1)S(1)} %broadcast_in_dim.42), channel_id=1, replica_groups=mesh['x'=4,'z'=8,'grp'=8] {'z'}, dimensions={0} | all-to-all | bytes 524288 | tf_op jit(solution)/shard_map/all_to_all | solution.py:147
  124.8 0.1 broadcast_in_dim.44
  124.9 13.3 %all_to_all.79.summed = bf16[4,256,512]{2,1,0:T(8,128)(2,1)S(1)} all-to-all(bf16[4,256,512]{2,1,0:T(8,128)(2,1)S(1)} %broadcast_in_dim.44), channel_id=1, replica_groups=mesh['x'=4,'z'=8,'grp'=8] {'x'}, dimensions={0} | all-to-all | bytes 2097152 | tf_op jit(solution)/shard_map/all_to_all | solution.py:148
  138.2 13.2 %shard_map.43 = bf16[4,256,512]{2,1,0:T(8,128)(2,1)S(1)} custom-call(bf16[4,256,512]{2,1,0:T(8,128)(2,1)S(1)} %all_to_all.79.summed, bf16[1024,2048]{1,0:T(8,128)(2,1)S(1)} %copy-done.2), custom_call_target="tpu_custom_call" | custom-call | tf_op jit(solution)/shard_map/pallas_call | solution.py:129
  151.4 13.3 %all_to_all.80 = bf16[4,256,512]{2,1,0:T(8,128)(2,1)S(1)} all-to-all(bf16[4,256,512]{2,1,0:T(8,128)(2,1)S(1)} %shard_map.43), channel_id=1, replica_groups=mesh['x'=4,'z'=8,'grp'=8] {'x'}, dimensions={0} | all-to-all | bytes 2097152 | tf_op jit(solution)/shard_map/all_to_all | solution.py:142
  164.7 0.2 reduce_sum.76
  165.0 15.4 %all_to_all.81 = bf16[8,32,512]{2,1,0:T(8,128)(2,1)S(1)} all-to-all(bf16[8,32,512]{2,1,0:T(8,128)(2,1)S(1)} %bitcast.18), channel_id=1, replica_groups=mesh['x'=4,'z'=8,'grp'=8] {'z'}, dimensions={0} | all-to-all | bytes 524288 | tf_op jit(solution)/shard_map/all_to_all | solution.py:144
  180.4 0.0 copy-start.3
  180.4 13.4 %all_to_all.82 = bf16[8,32,512]{2,1,0:T(8,128)(2,1)S(1)} all-to-all(bf16[8,32,512]{2,1,0:T(8,128)(2,1)S(1)} %broadcast_in_dim.45), channel_id=1, replica_groups=mesh['x'=4,'z'=8,'grp'=8] {'z'}, dimensions={0} | all-to-all | bytes 524288 | tf_op jit(solution)/shard_map/all_to_all | solution.py:147
  193.9 0.1 broadcast_in_dim.47
  193.9 13.3 %all_to_all.83.summed = bf16[4,256,512]{2,1,0:T(8,128)(2,1)S(1)} all-to-all(bf16[4,256,512]{2,1,0:T(8,128)(2,1)S(1)} %broadcast_in_dim.47), channel_id=1, replica_groups=mesh['x'=4,'z'=8,'grp'=8] {'x'}, dimensions={0} | all-to-all | bytes 2097152 | tf_op jit(solution)/shard_map/all_to_all | solution.py:148
  207.3 12.2 %shard_map.44 = (f32[2048,256]{1,0:T(8,128)}, bf16[1024,256]{1,0:T(8,128)(2,1)S(1)}) custom-call(bf16[4,256,512]{2,1,0:T(8,128)(2,1)S(1)} %all_to_all.83.summed, bf16[1024,2048]{1,0:T(8,128)(2,1)S(1)} %copy-done.3), custom_call_target="tpu_custom_call" | custom-call | tf_op jit(solution)/shard_map/pallas_call | solution.py:129
  219.5 17.6 %all_to_all.84 = bf16[32,32,256]{2,1,0:T(8,128)(2,1)S(1)} all-to-all(bf16[32,32,256]{2,1,0:T(8,128)(2,1)S(1)} %bitcast.11), channel_id=1, replica_groups=mesh['x'=4,'z'=8,'grp'=8] {'x','z'}, dimensions={0} | all-to-all | bytes 1048576 | tf_op jit(solution)/shard_map/all_to_all | solution.py:171
  237.1 0.8 copy.7
  (8 shorter events, 0.2 us)
Async XLA Ops:
  2.9 2.2 copy-start
  44.5 27.1 %copy-start.1 = (bf16[1024,2048]{1,0:T(8,128)(2,1)S(1)}, bf16[1024,2048]{1,0:T(8,128)(2,1)}, u32[]{:S(2)}) copy-start(bf16[1024,2048]{1,0:T(8,128)(2,1)} %keys_hbm.5) | copy-start | bytes 12582916
  111.5 26.7 %copy-start.2 = (bf16[1024,2048]{1,0:T(8,128)(2,1)S(1)}, bf16[1024,2048]{1,0:T(8,128)(2,1)}, u32[]{:S(2)}) copy-start(bf16[1024,2048]{1,0:T(8,128)(2,1)} %keys_hbm.5) | copy-start | bytes 12582916
  180.4 26.8 %copy-start.3 = (bf16[1024,2048]{1,0:T(8,128)(2,1)S(1)}, bf16[1024,2048]{1,0:T(8,128)(2,1)}, u32[]{:S(2)}) copy-start(bf16[1024,2048]{1,0:T(8,128)(2,1)} %keys_hbm.5) | copy-start | bytes 12582916

commit v2 on v1

--- a/solution.py
+++ b/solution.py
@@ -10,8 +10,10 @@
 
 ITERS = 3
 NX = 4
-NZ = 8
+NZ_HIGH = 4
+NZ_LOW = 2
 NB = 32
+AXES = ("x", "z_high", "z_low", "grp")
 VMEM_BYTES = 40 * 1024 * 1024
 F32 = jnp.float32
 BF16 = jnp.bfloat16
@@ -138,14 +140,19 @@
 
 def sum_and_spread(local_term):
     _, rank, width = local_term.shape
-    part = rank // NZ
-    terms = lax.all_to_all(local_term, "x", 0, 0, tiled=True)
-    total = jnp.sum(terms.astype(F32), axis=0).astype(BF16).reshape(NZ, part, width)
-    terms = lax.all_to_all(total, "z", 0, 0, tiled=True)
-    total = jnp.sum(terms.astype(F32), axis=0).astype(BF16)
-    total = jnp.broadcast_to(total[None], (NZ, part, width))
-    block = lax.all_to_all(total, "z", 0, 0, tiled=True).reshape(1, rank, width)
-    return lax.all_to_all(jnp.broadcast_to(block, (NX, rank, width)), "x", 0, 0, tiled=True)
+    near = NX * NZ_LOW
+    part = rank // NZ_LOW
+    terms = local_term.reshape(near, part, width)
+    terms = lax.all_to_all(terms, ("x", "z_low"), 0, 0, tiled=True)
+    own = jnp.sum(terms.astype(F32), axis=0).astype(BF16)
+    first, second, third = (
+        lax.ppermute(own, "z_high", [(i, (i + step) % NZ_HIGH) for i in range(NZ_HIGH)]).astype(F32)
+        for step in range(1, NZ_HIGH)
+    )
+    total = ((own.astype(F32) + second) + (first + third)).astype(BF16)
+    total = jnp.broadcast_to(total[None], (near, part, width))
+    blocks = lax.all_to_all(total, ("x", "z_low"), 0, 0, tiled=True)
+    return blocks.reshape(NX, rank, width)
 
 
 def local(key_cache, init_basis):
@@ -168,16 +175,16 @@
     summed = sum_and_spread(term)
     outs = (shape((features, rank), F32), shape((positions, rank), BF16))
     basis, compressed = call(last_kernel, outs, (summed, key_cache), (False, True), scratch)
-    latents = lax.all_to_all(compressed, ("x", "z"), split_axis=0, concat_axis=0, tiled=True)
+    latents = lax.all_to_all(compressed, ("x", "z_high", "z_low"), split_axis=0, concat_axis=0, tiled=True)
     return basis, latents
 
 
 def solution(mesh):
-    grid = Mesh(mesh.devices.reshape(NX, NZ, -1), ("x", "z", "grp"))
+    grid = Mesh(mesh.devices.reshape(NX, NZ_HIGH, NZ_LOW, -1), AXES)
     return jax.shard_map(
         local,
         mesh=grid,
-        in_specs=(P(("grp", "x", "z"), None), P("grp", None)),
-        out_specs=(P("grp", None), P(("grp", "x", "z"), None)),
+        in_specs=(P(("grp",) + AXES[:3], None), P("grp", None)),
+        out_specs=(P("grp", None), P(("grp",) + AXES[:3], None)),
         check_vma=False,
     )

time: 238 us -> 232 us (0.975)
  blocking collectives: 190 us -> 120 us
  starting transfers between devices: 0 us -> 29.5 us
  waiting for transfers between devices: 0 us -> 27.4 us
  local copies, waits for them, and re-layouts: 3.82 us -> 10.3 us
    all_to_all x13 -> x7, blocking collectives: 190 us -> 120 us  [the longest x3 48.4 us: sum_and_spread(): terms = lax.all_to_all(terms, ('x', 'z_low'), 0, 0, tiled=True)]
    ppermute x0 -> x9, starting transfers between devices: none -> 29.5 us  [sum_and_spread(): lax.ppermute(own, 'z_high', [(i, (i + step) % NZ_HIGH) for i in range(NZ_...]
    ppermute x0 -> x9, waiting for transfers between devices: none -> 27.4 us  [sum_and_spread(): lax.ppermute(own, 'z_high', [(i, (i + step) % NZ_HIGH) for i in range(NZ_...]
    unnamed x9, local copies, waits for them, and re-layouts: 3 us -> 9.54 us
  transfers between devices with their start and end apart: 0 -> 9, of which waited for: 0 -> 6; matrix products, arithmetic and copies ran while one was open for 0% -> 0% of each run, Pallas kernels for 0% -> 0%
where the time goes in v2:
time: 232 us; the launch traced here: 231 us
  blocking collectives  120 us (52%)
  Pallas kernels  41 us (18%)
  starting transfers between devices  29.5 us (13%)
  waiting for transfers between devices  27.4 us (12%)
  local copies, waits for them, and re-layouts  10.3 us (4%)
  other arithmetic  2.34 us (1%)
    all_to_all x3, blocking collectives, sum_and_spread(): terms = lax.all_to_all(terms, ('x', 'z_low'), 0, 0, tiled=True)  48.4 us
    all_to_all x3, blocking collectives, sum_and_spread(): blocks = lax.all_to_all(total, ('x', 'z_low'), 0, 0, tiled=True)  46.6 us
    pallas_call x4, Pallas kernels, call(): pl.pallas_call(body, out_shape=out_shape, in_specs=spec, out_specs=jax.tr...  41 us
    ppermute x9, starting transfers between devices, sum_and_spread(): lax.ppermute(own, 'z_high', [(i, (i + step) % NZ_HIGH) for i in range(NZ_...  29.5 us
    ppermute x9, waiting for transfers between devices, sum_and_spread(): lax.ppermute(own, 'z_high', [(i, (i + step) % NZ_HIGH) for i in range(NZ_...  27.4 us
    all_to_all x1, blocking collectives, local(): lax.all_to_all(compressed, ('x', 'z_high', 'z_low'), split_axis=0, concat...  25.2 us
    unnamed x9, local copies, waits for them, and re-layouts  9.54 us
  transfers between devices with their start and end apart: 9, of which 6 were waited for; matrix products, arithmetic and copies ran while one was open for 0% of the time, Pallas kernels for 0%

profile of v2, /device:TPU:56, one launch (start us, length us, event | category | flops | bytes accessed | tf_op | source)
XLA Modules:
  0.0 231.5 jit_solution(6385083179872397142)
XLA Ops:
  0.6 1.7 convert_element_type.54
  2.3 0.5 copy.4
  2.9 2.2 copy-done
  5.1 2.4 %shard_map.41 = bf16[4,256,512]{2,1,0:T(8,128)(2,1)S(1)} custom-call(bf16[1024,2048]{1,0:T(8,128)(2,1)S(1)} %copy-done, bf16[4,256,512]{2,1,0:T(8,128)(2,1)S(1)} %bitcast.11), custom_call_target="tpu_custom_call" | custom-call | tf_op jit(solution)/shard_map/pallas_call | solution.py:131
  7.4 20.1 %all_to_all.42 = bf16[8,128,512]{2,1,0:T(8,128)(2,1)S(1)} all-to-all(bf16[8,128,512]{2,1,0:T(8,128)(2,1)S(1)} %bitcast.12), channel_id=1, replica_groups=mesh['x'=4,'z_high'=4,'z_low'=2,'grp'=8] {'x','z_low'}, dimensions={0} | all-to-all | bytes 2097152 | tf_op jit(solution)/shard_map/all_to_all | solution.py:146
  27.5 0.1 reduce_sum.36
  27.7 5.5 %collective-permute-start.2 = (bf16[128,512]{1,0:T(8,128)(2,1)S(1)}, bf16[128,512]{1,0:T(8,128)(2,1)S(1)}, u32[]{:S(2)}, u32[]{:S(2)}) collective-permute-start(bf16[128,512]{1,0:T(8,128)(2,1)S(1)} %reduce_sum.36), channel_id=1, source_target_pairs={{0,48},{16,0},{32,16},{48,32},{1,49},{17,1},{33,17},{49,33},{2,50}... | collective-permute-start | bytes 393224 | tf_op jit(solution)/shard_map/ppermute | solution.py:149
  33.2 3.8 %collective-permute-start = (bf16[128,512]{1,0:T(8,128)(2,1)S(1)}, bf16[128,512]{1,0:T(8,128)(2,1)S(1)}, u32[]{:S(2)}, u32[]{:S(2)}) collective-permute-start(bf16[128,512]{1,0:T(8,128)(2,1)S(1)} %reduce_sum.36), channel_id=1, source_target_pairs={{0,32},{16,48},{32,0},{48,16},{1,33},{17,49},{33,1},{49,17},{2,34}... | collective-permute-start | bytes 393224 | tf_op jit(solution)/shard_map/ppermute | solution.py:149
  37.0 1.0 collective-permute-done.2
  38.0 9.4 %collective-permute-done.1 = bf16[128,512]{1,0:T(8,128)(2,1)S(1)} collective-permute-done((bf16[128,512]{1,0:T(8,128)(2,1)S(1)}, bf16[128,512]{1,0:T(8,128)(2,1)S(1)}, u32[]{:S(2)}, u32[]{:S(2)}) %collective-permute-start.1) | collective-permute-done | bytes 131104 | tf_op jit(solution)/shard_map/ppermute | solution.py:149
  47.5 15.4 %all_to_all.43 = bf16[8,128,512]{2,1,0:T(8,128)(2,1)S(1)} all-to-all(bf16[8,128,512]{2,1,0:T(8,128)(2,1)S(1)} %broadcast_in_dim.6), channel_id=1, replica_groups=mesh['x'=4,'z_high'=4,'z_low'=2,'grp'=8] {'x','z_low'}, dimensions={0} | all-to-all | bytes 2097152 | tf_op jit(solution)/shard_map/all_to_all | solution.py:154
  62.9 2.2 copy-done.1
  65.0 13.2 %shard_map.42 = bf16[4,256,512]{2,1,0:T(8,128)(2,1)S(1)} custom-call(bf16[4,256,512]{2,1,0:T(8,128)(2,1)S(1)} %bitcast.13, bf16[1024,2048]{1,0:T(8,128)(2,1)S(1)} %copy-done.1), custom_call_target="tpu_custom_call" | custom-call | tf_op jit(solution)/shard_map/pallas_call | solution.py:131
  78.2 14.3 %all_to_all.44 = bf16[8,128,512]{2,1,0:T(8,128)(2,1)S(1)} all-to-all(bf16[8,128,512]{2,1,0:T(8,128)(2,1)S(1)} %bitcast.14), channel_id=1, replica_groups=mesh['x'=4,'z_high'=4,'z_low'=2,'grp'=8] {'x','z_low'}, dimensions={0} | all-to-all | bytes 2097152 | tf_op jit(solution)/shard_map/all_to_all | solution.py:146
  92.6 7.3 %collective-permute-start.5 = (bf16[128,512]{1,0:T(8,128)(2,1)S(1)}, bf16[128,512]{1,0:T(8,128)(2,1)S(1)}, u32[]{:S(2)}, u32[]{:S(2)}) collective-permute-start(bf16[128,512]{1,0:T(8,128)(2,1)S(1)} %reduce_sum.37), channel_id=1, source_target_pairs={{0,48},{16,0},{32,16},{48,32},{1,49},{17,1},{33,17},{49,33},{2,50}... | collective-permute-start | bytes 393224 | tf_op jit(solution)/shard_map/ppermute | solution.py:149
  99.9 2.4 %collective-permute-start.3 = (bf16[128,512]{1,0:T(8,128)(2,1)S(1)}, bf16[128,512]{1,0:T(8,128)(2,1)S(1)}, u32[]{:S(2)}, u32[]{:S(2)}) collective-permute-start(bf16[128,512]{1,0:T(8,128)(2,1)S(1)} %reduce_sum.37), channel_id=1, source_target_pairs={{0,32},{16,48},{32,0},{48,16},{1,33},{17,49},{33,1},{49,17},{2,34}... | collective-permute-start | bytes 393224 | tf_op jit(solution)/shard_map/ppermute | solution.py:149
  102.4 1.5 collective-permute-done.5
  103.9 9.2 %collective-permute-done.4 = bf16[128,512]{1,0:T(8,128)(2,1)S(1)} collective-permute-done((bf16[128,512]{1,0:T(8,128)(2,1)S(1)}, bf16[128,512]{1,0:T(8,128)(2,1)S(1)}, u32[]{:S(2)}, u32[]{:S(2)}) %collective-permute-start.4) | collective-permute-done | bytes 131104 | tf_op jit(solution)/shard_map/ppermute | solution.py:149
  113.2 15.6 %all_to_all.45 = bf16[8,128,512]{2,1,0:T(8,128)(2,1)S(1)} all-to-all(bf16[8,128,512]{2,1,0:T(8,128)(2,1)S(1)} %broadcast_in_dim.7), channel_id=1, replica_groups=mesh['x'=4,'z_high'=4,'z_low'=2,'grp'=8] {'x','z_low'}, dimensions={0} | all-to-all | bytes 2097152 | tf_op jit(solution)/shard_map/all_to_all | solution.py:154
  128.9 2.2 copy-done.2
  131.1 13.2 %shard_map.43 = bf16[4,256,512]{2,1,0:T(8,128)(2,1)S(1)} custom-call(bf16[4,256,512]{2,1,0:T(8,128)(2,1)S(1)} %bitcast.15, bf16[1024,2048]{1,0:T(8,128)(2,1)S(1)} %copy-done.2), custom_call_target="tpu_custom_call" | custom-call | tf_op jit(solution)/shard_map/pallas_call | solution.py:131
  144.2 14.0 %all_to_all.46 = bf16[8,128,512]{2,1,0:T(8,128)(2,1)S(1)} all-to-all(bf16[8,128,512]{2,1,0:T(8,128)(2,1)S(1)} %bitcast.16), channel_id=1, replica_groups=mesh['x'=4,'z_high'=4,'z_low'=2,'grp'=8] {'x','z_low'}, dimensions={0} | all-to-all | bytes 2097152 | tf_op jit(solution)/shard_map/all_to_all | solution.py:146
  158.4 4.4 %collective-permute-start.8 = (bf16[128,512]{1,0:T(8,128)(2,1)S(1)}, bf16[128,512]{1,0:T(8,128)(2,1)S(1)}, u32[]{:S(2)}, u32[]{:S(2)}) collective-permute-start(bf16[128,512]{1,0:T(8,128)(2,1)S(1)} %reduce_sum.38), channel_id=1, source_target_pairs={{0,48},{16,0},{32,16},{48,32},{1,49},{17,1},{33,17},{49,33},{2,50}... | collective-permute-start | bytes 393224 | tf_op jit(solution)/shard_map/ppermute | solution.py:149
  162.9 2.5 %collective-permute-start.7 = (bf16[128,512]{1,0:T(8,128)(2,1)S(1)}, bf16[128,512]{1,0:T(8,128)(2,1)S(1)}, u32[]{:S(2)}, u32[]{:S(2)}) collective-permute-start(bf16[128,512]{1,0:T(8,128)(2,1)S(1)} %reduce_sum.38), channel_id=1, source_target_pairs={{0,16},{16,32},{32,48},{48,0},{1,17},{17,33},{33,49},{49,1},{2,18}... | collective-permute-start | bytes 393224 | tf_op jit(solution)/shard_map/ppermute | solution.py:149
  165.4 3.5 %collective-permute-start.6 = (bf16[128,512]{1,0:T(8,128)(2,1)S(1)}, bf16[128,512]{1,0:T(8,128)(2,1)S(1)}, u32[]{:S(2)}, u32[]{:S(2)}) collective-permute-start(bf16[128,512]{1,0:T(8,128)(2,1)S(1)} %reduce_sum.38), channel_id=1, source_target_pairs={{0,32},{16,48},{32,0},{48,16},{1,33},{17,49},{33,1},{49,17},{2,34}... | collective-permute-start | bytes 393224 | tf_op jit(solution)/shard_map/ppermute | solution.py:149
  168.9 3.1 %collective-permute-done.8 = bf16[128,512]{1,0:T(8,128)(2,1)S(1)} collective-permute-done((bf16[128,512]{1,0:T(8,128)(2,1)S(1)}, bf16[128,512]{1,0:T(8,128)(2,1)S(1)}, u32[]{:S(2)}, u32[]{:S(2)}) %collective-permute-start.8) | collective-permute-done | bytes 131104 | tf_op jit(solution)/shard_map/ppermute | solution.py:149
  172.0 3.3 %collective-permute-done.6 = bf16[128,512]{1,0:T(8,128)(2,1)S(1)} collective-permute-done((bf16[128,512]{1,0:T(8,128)(2,1)S(1)}, bf16[128,512]{1,0:T(8,128)(2,1)S(1)}, u32[]{:S(2)}, u32[]{:S(2)}) %collective-permute-start.6) | collective-permute-done | bytes 131104 | tf_op jit(solution)/shard_map/ppermute | solution.py:149
  175.4 15.6 %all_to_all.47 = bf16[8,128,512]{2,1,0:T(8,128)(2,1)S(1)} all-to-all(bf16[8,128,512]{2,1,0:T(8,128)(2,1)S(1)} %broadcast_in_dim.8), channel_id=1, replica_groups=mesh['x'=4,'z_high'=4,'z_low'=2,'grp'=8] {'x','z_low'}, dimensions={0} | all-to-all | bytes 2097152 | tf_op jit(solution)/shard_map/all_to_all | solution.py:154
  191.1 2.2 copy-done.3
  193.2 12.3 %shard_map.44 = (f32[2048,256]{1,0:T(8,128)}, bf16[1024,256]{1,0:T(8,128)(2,1)S(1)}) custom-call(bf16[4,256,512]{2,1,0:T(8,128)(2,1)S(1)} %bitcast.10, bf16[1024,2048]{1,0:T(8,128)(2,1)S(1)} %copy-done.3), custom_call_target="tpu_custom_call" | custom-call | tf_op jit(solution)/shard_map/pallas_call | solution.py:131
  205.5 25.2 %all_to_all.48 = bf16[32,32,256]{2,1,0:T(8,128)(2,1)S(1)} all-to-all(bf16[32,32,256]{2,1,0:T(8,128)(2,1)S(1)} %bitcast.17), channel_id=1, replica_groups=mesh['x'=4,'z_high'=4,'z_low'=2,'grp'=8] {'x','z_high','z_low'}, dimensions={0} | all-to-all | bytes 1048576 | tf_op jit(solution)/shard_map/all_to_all | solution.py:178
  230.7 0.8 copy.6
  (17 shorter events, 0.8 us)
Async XLA Ops:
  2.9 2.2 copy-start
  27.7 10.3 %collective-permute-start.2 = (bf16[128,512]{1,0:T(8,128)(2,1)S(1)}, bf16[128,512]{1,0:T(8,128)(2,1)S(1)}, u32[]{:S(2)}, u32[]{:S(2)}) collective-permute-start(bf16[128,512]{1,0:T(8,128)(2,1)S(1)} %reduce_sum.36), channel_id=1, source_target_pairs={{0,48},{16,0},{32,16},{48,32},{1,49},{17,1},{33,17},{49,33},{2,50}... | collective-permute-start | bytes 393224 | tf_op jit(solution)/shard_map/ppermute | solution.py:149
  33.2 14.2 %collective-permute-start.1 = (bf16[128,512]{1,0:T(8,128)(2,1)S(1)}, bf16[128,512]{1,0:T(8,128)(2,1)S(1)}, u32[]{:S(2)}, u32[]{:S(2)}) collective-permute-start(bf16[128,512]{1,0:T(8,128)(2,1)S(1)} %reduce_sum.36), channel_id=1, source_target_pairs={{0,16},{16,32},{32,48},{48,0},{1,17},{17,33},{33,49},{49,1},{2,18}... | collective-permute-start | bytes 393224 | tf_op jit(solution)/shard_map/ppermute | solution.py:149
  33.2 14.2 %collective-permute-start = (bf16[128,512]{1,0:T(8,128)(2,1)S(1)}, bf16[128,512]{1,0:T(8,128)(2,1)S(1)}, u32[]{:S(2)}, u32[]{:S(2)}) collective-permute-start(bf16[128,512]{1,0:T(8,128)(2,1)S(1)} %reduce_sum.36), channel_id=1, source_target_pairs={{0,32},{16,48},{32,0},{48,16},{1,33},{17,49},{33,1},{49,17},{2,34}... | collective-permute-start | bytes 393224 | tf_op jit(solution)/shard_map/ppermute | solution.py:149
  62.9 2.2 copy-start.1
  92.6 11.3 %collective-permute-start.5 = (bf16[128,512]{1,0:T(8,128)(2,1)S(1)}, bf16[128,512]{1,0:T(8,128)(2,1)S(1)}, u32[]{:S(2)}, u32[]{:S(2)}) collective-permute-start(bf16[128,512]{1,0:T(8,128)(2,1)S(1)} %reduce_sum.37), channel_id=1, source_target_pairs={{0,48},{16,0},{32,16},{48,32},{1,49},{17,1},{33,17},{49,33},{2,50}... | collective-permute-start | bytes 393224 | tf_op jit(solution)/shard_map/ppermute | solution.py:149
  99.9 13.2 %collective-permute-start.4 = (bf16[128,512]{1,0:T(8,128)(2,1)S(1)}, bf16[128,512]{1,0:T(8,128)(2,1)S(1)}, u32[]{:S(2)}, u32[]{:S(2)}) collective-permute-start(bf16[128,512]{1,0:T(8,128)(2,1)S(1)} %reduce_sum.37), channel_id=1, source_target_pairs={{0,16},{16,32},{32,48},{48,0},{1,17},{17,33},{33,49},{49,1},{2,18}... | collective-permute-start | bytes 393224 | tf_op jit(solution)/shard_map/ppermute | solution.py:149
  99.9 13.2 %collective-permute-start.3 = (bf16[128,512]{1,0:T(8,128)(2,1)S(1)}, bf16[128,512]{1,0:T(8,128)(2,1)S(1)}, u32[]{:S(2)}, u32[]{:S(2)}) collective-permute-start(bf16[128,512]{1,0:T(8,128)(2,1)S(1)} %reduce_sum.37), channel_id=1, source_target_pairs={{0,32},{16,48},{32,0},{48,16},{1,33},{17,49},{33,1},{49,17},{2,34}... | collective-permute-start | bytes 393224 | tf_op jit(solution)/shard_map/ppermute | solution.py:149
  128.9 2.2 copy-start.2
  158.4 13.6 %collective-permute-start.8 = (bf16[128,512]{1,0:T(8,128)(2,1)S(1)}, bf16[128,512]{1,0:T(8,128)(2,1)S(1)}, u32[]{:S(2)}, u32[]{:S(2)}) collective-permute-start(bf16[128,512]{1,0:T(8,128)(2,1)S(1)} %reduce_sum.38), channel_id=1, source_target_pairs={{0,48},{16,0},{32,16},{48,32},{1,49},{17,1},{33,17},{49,33},{2,50}... | collective-permute-start | bytes 393224 | tf_op jit(solution)/shard_map/ppermute | solution.py:149
  162.9 9.1 %collective-permute-start.7 = (bf16[128,512]{1,0:T(8,128)(2,1)S(1)}, bf16[128,512]{1,0:T(8,128)(2,1)S(1)}, u32[]{:S(2)}, u32[]{:S(2)}) collective-permute-start(bf16[128,512]{1,0:T(8,128)(2,1)S(1)} %reduce_sum.38), channel_id=1, source_target_pairs={{0,16},{16,32},{32,48},{48,0},{1,17},{17,33},{33,49},{49,1},{2,18}... | collective-permute-start | bytes 393224 | tf_op jit(solution)/shard_map/ppermute | solution.py:149
  165.4 9.9 %collective-permute-start.6 = (bf16[128,512]{1,0:T(8,128)(2,1)S(1)}, bf16[128,512]{1,0:T(8,128)(2,1)S(1)}, u32[]{:S(2)}, u32[]{:S(2)}) collective-permute-start(bf16[128,512]{1,0:T(8,128)(2,1)S(1)} %reduce_sum.38), channel_id=1, source_target_pairs={{0,32},{16,48},{32,0},{48,16},{1,33},{17,49},{33,1},{49,17},{2,34}... | collective-permute-start | bytes 393224 | tf_op jit(solution)/shard_map/ppermute | solution.py:149
  191.0 2.2 copy-start.3

commit v3 on v2

v3 whole, which is shorter than its diff:
```python
import jax
import jax.numpy as jnp
from jax import lax
from jax.experimental import pallas as pl
from jax.experimental.pallas import tpu as pltpu
from jax.sharding import Mesh
from jax.sharding import PartitionSpec as P

ITERS = 3
NX = 4
NZ_HIGH = 4
NZ_LOW = 2
NB = 32
GROUP = 8
STRIP = 16
AXES = ("x", "z_high", "z_low", "grp")
VMEM_BYTES = 59_500_000
F32 = jnp.float32
BF16 = jnp.bfloat16

NN = (((1,), (0,)), ((), ()))
NT = (((1,), (1,)), ((), ()))
TN = (((0,), (0,)), ((), ()))


def dot(a, b, dims):
    return lax.dot_general(a, b, dims, preferred_element_type=F32)


def split(a):
    high = a.astype(BF16)
    rest = a - high.astype(F32)
    mid = rest.astype(BF16)
    low = (rest - mid.astype(F32)).astype(BF16)
    return high, mid, low


def stacked(parts, order):
    return jnp.concatenate([parts[i] for i in order], axis=0)


LEFT = (0, 0, 1, 0, 2, 1)
RIGHT = (0, 1, 0, 2, 0, 1)


def widen(a, lanes):
    return jnp.concatenate([a] * (lanes // 128), axis=1) if lanes > 128 else a


def eliminate(rows, inverse, column):
    row_id = lax.broadcasted_iota(jnp.int32, (GROUP, 128), 0)
    groups = len(rows)
    rows, inverse = list(rows), list(inverse)
    lanes, inverse_lanes = rows[0].shape[1], inverse[0].shape[1]
    for first in range(0, groups, STRIP // GROUP):
        held = {}
        for g in range(first, groups):
            at = column + first * GROUP
            held[g] = [
                jnp.broadcast_to(rows[g][:, at + s : at + s + 1], (GROUP, 128)) for s in range(STRIP)
            ]
        for s in range(STRIP):
            own, k = first + s // GROUP, s % GROUP
            if k == 0:
                pivots = jnp.ones((GROUP, 128), F32)
            pivot = held[own][s][k : k + 1, :]
            reciprocal = 1.0 / pivot
            pivots = jnp.where(row_id == k, pivot, pivots)
            heads = [held[own][t][k : k + 1, :] * reciprocal for t in range(s + 1, STRIP)]
            pivot_row, pivot_inverse = rows[own][k : k + 1, :], inverse[own][k : k + 1, :]
            for g in range(own, groups):
                base = held[g][s]
                for t in range(s + 1, STRIP):
                    held[g][t] = held[g][t] - base * heads[t - s - 1]
                factor = base * reciprocal
                if g == own:
                    factor = jnp.where(row_id > k, factor, 0.0)
                rows[g] = rows[g] - widen(factor, lanes) * pivot_row
                inverse[g] = inverse[g] - widen(factor, inverse_lanes) * pivot_inverse
            if k == GROUP - 1:
                scale = lax.rsqrt(pivots)
                rows[own] = rows[own] * widen(scale, lanes)
                inverse[own] = inverse[own] * widen(scale, inverse_lanes)
    return rows, inverse


def inverse_factor(gram, inv):
    n = gram.shape[0]
    eye = lax.broadcasted_iota(jnp.int32, (n, n), 0) == lax.broadcasted_iota(jnp.int32, (n, n), 1)
    inv[...] = eye.astype(F32)
    for start in range(0, n, NB):
        done = start + NB
        left = start // 128 * 128
        right = -(-done // 128) * 128
        groups = [pl.ds(start + g, GROUP) for g in range(0, NB, GROUP)]
        upper, lower = eliminate(
            [gram[g, left:] for g in groups], [inv[g, :right] for g in groups], start - left
        )
        upper, lower = jnp.concatenate(upper, axis=0), jnp.concatenate(lower, axis=0)
        inv[pl.ds(start, NB), :right] = lower
        if done < n:
            keep = done // 128 * 128
            upper_parts = split(upper[:, keep - left :])
            factor = stacked(upper_parts, LEFT)
            rest = pl.ds(done, n - done)
            update = dot(factor, stacked(upper_parts, RIGHT), TN)
            gram[rest, keep:] = gram[rest, keep:] - update[done - keep :]
            update = dot(factor, stacked(split(lower), RIGHT), TN)
            inv[rest, :right] = inv[rest, :right] - update[done - keep :]


def products(keys, basis, out):
    width = basis[0].shape[1]
    projected = 0.0
    for x in range(NX):
        projected = projected + dot(basis[x], keys[:, x * width : (x + 1) * width], NT)
    projected = projected.astype(BF16)
    for x in range(NX):
        out[x] = dot(projected, keys[:, x * width : (x + 1) * width], NN).astype(BF16)


def first_kernel(keys_hbm, basis_hbm, out, keys, basis, key_sems, basis_sems):
    width = keys.shape[1] // NX
    copies = []
    for x in range(NX):
        part = pl.ds(x * width, width)
        of_basis = pltpu.make_async_copy(basis_hbm.at[part, :], basis.at[part, :], basis_sems.at[x])
        of_keys = pltpu.make_async_copy(keys_hbm.at[:, part], keys.at[:, part], key_sems.at[x])
        of_basis.start()
        of_keys.start()
        copies.append((of_basis, of_keys))
    projected = 0.0
    for x, (of_basis, of_keys) in enumerate(copies):
        of_basis.wait()
        rounded = basis[pl.ds(x * width, width), :].T.astype(BF16)
        of_keys.wait()
        projected = projected + dot(rounded, keys[:, x * width : (x + 1) * width], NT)
    projected = projected.astype(BF16)
    for x in range(NX):
        out[x] = dot(projected, keys[:, x * width : (x + 1) * width], NN).astype(BF16)


def basis_blocks(summed, inv):
    high, mid, _ = split(inv)
    return [dot(high, summed[x], NN) + dot(mid, summed[x], NN) for x in range(NX)]


def factorize(summed, gram, inv):
    total = 0.0
    for x in range(NX):
        total = total + dot(summed[x], summed[x], NT)
    gram[...] = total
    inverse_factor(gram, inv)


def middle_kernel(summed, keys_hbm, out, gram, inv, keys, sem):
    copy = pltpu.make_async_copy(keys_hbm, keys, sem)
    copy.start()
    factorize(summed, gram, inv)
    basis = [b.astype(BF16) for b in basis_blocks(summed, inv[...])]
    copy.wait()
    products(keys, basis, out)


def last_kernel(summed, keys_hbm, inv, out, gram, keys, sem):
    copy = pltpu.make_async_copy(keys_hbm, keys, sem)
    copy.start()
    factorize(summed, gram, inv)
    width = summed.shape[2]
    basis = [b.astype(BF16) for b in basis_blocks(summed, inv[...])]
    copy.wait()
    compressed = 0.0
    for x in range(NX):
        compressed = compressed + dot(keys[:, x * width : (x + 1) * width], basis[x], NT)
    out[...] = compressed.astype(BF16)


def basis_kernel(summed, inv, out):
    width = summed.shape[2]
    scale = jnp.sqrt(F32(NX * width))
    for x, block in enumerate(basis_blocks(summed, inv[...])):
        out[pl.ds(x * width, width), :] = (block * scale).T


def call(body, out_shape, operands, in_hbm, scratch, cost=None):
    spec = [pl.BlockSpec(memory_space=pl.ANY if h else pltpu.VMEM) for h in in_hbm]
    return pl.pallas_call(
        body,
        out_shape=out_shape,
        in_specs=spec,
        out_specs=jax.tree.map(lambda _: pl.BlockSpec(memory_space=pltpu.VMEM), out_shape),
        scratch_shapes=scratch,
        cost_estimate=cost,
        compiler_params=pltpu.CompilerParams(vmem_limit_bytes=VMEM_BYTES),
    )(*operands)


def add_up(terms):
    terms = [terms[i].astype(F32) for i in range(terms.shape[0])]
    while len(terms) > 1:
        terms = [a + b for a, b in zip(terms[0::2], terms[1::2])]
    return terms[0].astype(BF16)


def sum_and_spread(local_term):
    _, rank, width = local_term.shape
    near = NX * NZ_LOW
    part = rank // NZ_LOW
    terms = local_term.reshape(near, part, width)
    own = add_up(lax.all_to_all(terms, ("x", "z_low"), 0, 0, tiled=True))
    first, second, third = (
        lax.ppermute(own, "z_high", [(i, (i + step) % NZ_HIGH) for i in range(NZ_HIGH)]).astype(F32)
        for step in range(1, NZ_HIGH)
    )
    total = ((own.astype(F32) + second) + (first + third)).astype(BF16)
    total = jnp.broadcast_to(total[None], (near, part, width))
    blocks = lax.all_to_all(total, ("x", "z_low"), 0, 0, tiled=True)
    return blocks.reshape(NX, rank, width)


def local(key_cache, init_basis):
    positions, features = key_cache.shape
    rank = init_basis.shape[1]
    width = features // NX
    shape = jax.ShapeDtypeStruct
    square = pltpu.VMEM((rank, rank), F32)
    keys = pltpu.VMEM((positions, features), BF16)
    sem = pltpu.SemaphoreType.DMA
    blocks = shape((NX, rank, width), BF16)

    scratch = [keys, pltpu.VMEM((features, rank), F32), sem((NX,)), sem((NX,))]
    term = call(first_kernel, blocks, (key_cache, init_basis), (True, True), scratch)
    for sweep in range(ITERS - 1):
        summed = sum_and_spread(term)
        scratch = [square, square, keys, sem]
        term = call(middle_kernel, blocks, (summed, key_cache), (False, True), scratch)
    summed = sum_and_spread(term)
    outs = (shape((rank, rank), F32), shape((positions, rank), BF16))
    inv, compressed = call(
        last_kernel, outs, (summed, key_cache), (False, True), [square, keys, sem]
    )
    latents = lax.all_to_all(
        compressed, ("x", "z_high", "z_low"), split_axis=0, concat_axis=0, tiled=True
    )
    cost = pl.CostEstimate(
        flops=4 * rank * rank * features, bytes_accessed=8 * features * rank, transcendentals=0
    )
    basis = call(basis_kernel, shape((features, rank), F32), (summed, inv), (False, False), [], cost)
    return basis, latents


def solution(mesh):
    grid = Mesh(mesh.devices.reshape(NX, NZ_HIGH, NZ_LOW, -1), AXES)
    return jax.shard_map(
        local,
        mesh=grid,
        in_specs=(P(("grp",) + AXES[:3], None), P("grp", None)),
        out_specs=(P("grp", None), P(("grp",) + AXES[:3], None)),
        check_vma=False,
    )
```

time: 232 us -> 233 us (level)
  local copies, waits for them, and re-layouts: 10.3 us -> 1.04 us
  starting transfers between devices: 29.5 us -> 35.4 us
  blocking collectives: 120 us -> 123 us
    all_to_all x3, blocking collectives: 46.6 us -> 65.8 us  [sum_and_spread(): blocks = lax.all_to_all(total, ('x', 'z_low'), 0, 0, tiled=True)]
    all_to_all x4 -> x3, blocking collectives: 73.6 us -> 57.2 us  [sum_and_spread(): own = add_up(lax.all_to_all(terms, ('x', 'z_low'), 0, 0, tiled=True))]
    all_to_all x0 -> x1, waiting for transfers between devices: none -> 13.3 us  [local(): lax.all_to_all(compressed, ('x', 'z_high', 'z_low'), split_axis=0, concat...]
    ppermute x9, waiting for transfers between devices: 27.4 us -> 14.7 us  [sum_and_spread(): lax.ppermute(own, 'z_high', [(i, (i + step) % NZ_HIGH) for i in range(NZ_...]
    unnamed x9 -> x1, local copies, waits for them, and re-layouts: 9.54 us -> 0.79 us
    all_to_all x0 -> x1, starting transfers between devices: none -> 7.42 us  [local(): lax.all_to_all(compressed, ('x', 'z_high', 'z_low'), split_axis=0, concat...]
    pallas_call x4 -> x5, Pallas kernels: 41 us -> 43.3 us  [call(): pl.pallas_call(body, out_shape=out_shape, in_specs=spec, out_specs=jax.tr...]
  transfers between devices with their start and end apart: 9 -> 10, of which waited for: 6 -> 9; matrix products, arithmetic and copies ran while one was open for 0% -> 0% of each run, Pallas kernels for 0% -> 1%
where the time goes in v3:
time: 233 us; the launch traced here: 232 us
  blocking collectives  123 us (53%)
  Pallas kernels  43.3 us (19%)
  starting transfers between devices  35.4 us (15%)
  waiting for transfers between devices  27.9 us (12%)
    all_to_all x3, blocking collectives, sum_and_spread(): blocks = lax.all_to_all(total, ('x', 'z_low'), 0, 0, tiled=True)  65.8 us
    all_to_all x3, blocking collectives, sum_and_spread(): own = add_up(lax.all_to_all(terms, ('x', 'z_low'), 0, 0, tiled=True))  57.2 us
    pallas_call x5, Pallas kernels, call(): pl.pallas_call(body, out_shape=out_shape, in_specs=spec, out_specs=jax.tr...  43.3 us
    ppermute x9, starting transfers between devices, sum_and_spread(): lax.ppermute(own, 'z_high', [(i, (i + step) % NZ_HIGH) for i in range(NZ_...  28 us
    ppermute x9, waiting for transfers between devices, sum_and_spread(): lax.ppermute(own, 'z_high', [(i, (i + step) % NZ_HIGH) for i in range(NZ_...  14.7 us
    all_to_all x1, waiting for transfers between devices, local(): lax.all_to_all(compressed, ('x', 'z_high', 'z_low'), split_axis=0, concat...  13.3 us
    all_to_all x1, starting transfers between devices, local(): lax.all_to_all(compressed, ('x', 'z_high', 'z_low'), split_axis=0, concat...  7.42 us
  transfers between devices with their start and end apart: 10, of which 9 were waited for; matrix products, arithmetic and copies ran while one was open for 0% of the time, Pallas kernels for 1%

profile of v3, /device:TPU:56, one launch (start us, length us, event | category | flops | bytes accessed | tf_op | source)
XLA Modules:
  0.0 232.3 jit_solution(1545133730119681916)
XLA Ops:
  0.6 5.7 %shard_map.41 = bf16[4,256,512]{2,1,0:T(8,128)(2,1)} custom-call(bf16[1024,2048]{1,0:T(8,128)(2,1)} %keys_hbm.7, f32[2048,256]{1,0:T(8,128)} %basis_hbm.1), custom_call_target="tpu_custom_call" | custom-call | tf_op jit(solution)/shard_map/pallas_call | solution.py:187
  6.4 20.3 %all_to_all.42 = bf16[8,128,512]{2,1,0:T(8,128)(2,1)S(1)} all-to-all(bf16[8,128,512]{2,1,0:T(8,128)(2,1)} %bitcast.22), channel_id=1, replica_groups=mesh['x'=4,'z_high'=4,'z_low'=2,'grp'=8] {'x','z_low'}, dimensions={0} | all-to-all | bytes 2097152 | tf_op jit(solution)/shard_map/all_to_all | solution.py:210
  26.8 3.4 %collective-permute-start.1 = (bf16[128,512]{1,0:T(8,128)(2,1)S(1)}, bf16[128,512]{1,0:T(8,128)(2,1)S(1)}, u32[]{:S(2)}, u32[]{:S(2)}) collective-permute-start(bf16[128,512]{1,0:T(8,128)(2,1)S(1)} %fusion), channel_id=1, source_target_pairs={{0,16},{16,32},{32,48},{48,0},{1,17},{17,33},{33,49},{49,1},{2,18}... | collective-permute-start | bytes 393224 | tf_op jit(solution)/shard_map/ppermute | solution.py:212
  30.2 4.5 %collective-permute-start = (bf16[128,512]{1,0:T(8,128)(2,1)S(1)}, bf16[128,512]{1,0:T(8,128)(2,1)S(1)}, u32[]{:S(2)}, u32[]{:S(2)}) collective-permute-start(bf16[128,512]{1,0:T(8,128)(2,1)S(1)} %fusion), channel_id=1, source_target_pairs={{0,32},{16,48},{32,0},{48,16},{1,33},{17,49},{33,1},{49,17},{2,34}... | collective-permute-start | bytes 393224 | tf_op jit(solution)/shard_map/ppermute | solution.py:212
  34.6 2.7 %collective-permute-start.2 = (bf16[128,512]{1,0:T(8,128)(2,1)S(1)}, bf16[128,512]{1,0:T(8,128)(2,1)S(1)}, u32[]{:S(2)}, u32[]{:S(2)}) collective-permute-start(bf16[128,512]{1,0:T(8,128)(2,1)S(1)} %fusion), channel_id=1, source_target_pairs={{0,48},{16,0},{32,16},{48,32},{1,49},{17,1},{33,17},{49,33},{2,50}... | collective-permute-start | bytes 393224 | tf_op jit(solution)/shard_map/ppermute | solution.py:212
  37.3 0.2 collective-permute-done.1
  37.5 4.5 %collective-permute-done = bf16[128,512]{1,0:T(8,128)(2,1)S(1)} collective-permute-done((bf16[128,512]{1,0:T(8,128)(2,1)S(1)}, bf16[128,512]{1,0:T(8,128)(2,1)S(1)}, u32[]{:S(2)}, u32[]{:S(2)}) %collective-permute-start) | collective-permute-done | bytes 131104 | tf_op jit(solution)/shard_map/ppermute | solution.py:212
  42.0 1.0 collective-permute-done.2
  43.0 0.2 add_convert_fusion.4
  43.3 21.4 %all_to_all.43 = bf16[8,128,512]{2,1,0:T(8,128)(2,1)} all-to-all(bf16[8,128,512]{2,1,0:T(8,128)(2,1)S(1)} %broadcast_in_dim.6), channel_id=1, replica_groups=mesh['x'=4,'z_high'=4,'z_low'=2,'grp'=8] {'x','z_low'}, dimensions={0} | all-to-all | bytes 2097152 | tf_op jit(solution)/shard_map/all_to_all | solution.py:217
  64.6 11.8 %shard_map.42 = bf16[4,256,512]{2,1,0:T(8,128)(2,1)} custom-call(bf16[4,256,512]{2,1,0:T(8,128)(2,1)} %bitcast.23, bf16[1024,2048]{1,0:T(8,128)(2,1)} %keys_hbm.7), custom_call_target="tpu_custom_call" | custom-call | tf_op jit(solution)/shard_map/pallas_call | solution.py:187
  76.5 18.4 %all_to_all.44 = bf16[8,128,512]{2,1,0:T(8,128)(2,1)S(1)} all-to-all(bf16[8,128,512]{2,1,0:T(8,128)(2,1)} %bitcast.24), channel_id=1, replica_groups=mesh['x'=4,'z_high'=4,'z_low'=2,'grp'=8] {'x','z_low'}, dimensions={0} | all-to-all | bytes 2097152 | tf_op jit(solution)/shard_map/all_to_all | solution.py:210
  95.1 2.4 %collective-permute-start.4 = (bf16[128,512]{1,0:T(8,128)(2,1)S(1)}, bf16[128,512]{1,0:T(8,128)(2,1)S(1)}, u32[]{:S(2)}, u32[]{:S(2)}) collective-permute-start(bf16[128,512]{1,0:T(8,128)(2,1)S(1)} %fusion.1), channel_id=1, source_target_pairs={{0,16},{16,32},{32,48},{48,0},{1,17},{17,33},{33,49},{49,1},{2,18}... | collective-permute-start | bytes 393224 | tf_op jit(solution)/shard_map/ppermute | solution.py:212
  97.4 3.7 %collective-permute-start.3 = (bf16[128,512]{1,0:T(8,128)(2,1)S(1)}, bf16[128,512]{1,0:T(8,128)(2,1)S(1)}, u32[]{:S(2)}, u32[]{:S(2)}) collective-permute-start(bf16[128,512]{1,0:T(8,128)(2,1)S(1)} %fusion.1), channel_id=1, source_target_pairs={{0,32},{16,48},{32,0},{48,16},{1,33},{17,49},{33,1},{49,17},{2,34}... | collective-permute-start | bytes 393224 | tf_op jit(solution)/shard_map/ppermute | solution.py:212
  101.1 2.8 %collective-permute-start.5 = (bf16[128,512]{1,0:T(8,128)(2,1)S(1)}, bf16[128,512]{1,0:T(8,128)(2,1)S(1)}, u32[]{:S(2)}, u32[]{:S(2)}) collective-permute-start(bf16[128,512]{1,0:T(8,128)(2,1)S(1)} %fusion.1), channel_id=1, source_target_pairs={{0,48},{16,0},{32,16},{48,32},{1,49},{17,1},{33,17},{49,33},{2,50}... | collective-permute-start | bytes 393224 | tf_op jit(solution)/shard_map/ppermute | solution.py:212
  103.9 3.2 %collective-permute-done.3 = bf16[128,512]{1,0:T(8,128)(2,1)S(1)} collective-permute-done((bf16[128,512]{1,0:T(8,128)(2,1)S(1)}, bf16[128,512]{1,0:T(8,128)(2,1)S(1)}, u32[]{:S(2)}, u32[]{:S(2)}) %collective-permute-start.3) | collective-permute-done | bytes 131104 | tf_op jit(solution)/shard_map/ppermute | solution.py:212
  107.1 1.2 collective-permute-done.5
  108.6 22.2 %all_to_all.45 = bf16[8,128,512]{2,1,0:T(8,128)(2,1)} all-to-all(bf16[8,128,512]{2,1,0:T(8,128)(2,1)S(1)} %broadcast_in_dim.7), channel_id=1, replica_groups=mesh['x'=4,'z_high'=4,'z_low'=2,'grp'=8] {'x','z_low'}, dimensions={0} | all-to-all | bytes 2097152 | tf_op jit(solution)/shard_map/all_to_all | solution.py:217
  130.8 11.8 %shard_map.43 = bf16[4,256,512]{2,1,0:T(8,128)(2,1)} custom-call(bf16[4,256,512]{2,1,0:T(8,128)(2,1)} %bitcast.25, bf16[1024,2048]{1,0:T(8,128)(2,1)} %keys_hbm.7), custom_call_target="tpu_custom_call" | custom-call | tf_op jit(solution)/shard_map/pallas_call | solution.py:187
  142.6 18.5 %all_to_all.46 = bf16[8,128,512]{2,1,0:T(8,128)(2,1)S(1)} all-to-all(bf16[8,128,512]{2,1,0:T(8,128)(2,1)} %bitcast.26), channel_id=1, replica_groups=mesh['x'=4,'z_high'=4,'z_low'=2,'grp'=8] {'x','z_low'}, dimensions={0} | all-to-all | bytes 2097152 | tf_op jit(solution)/shard_map/all_to_all | solution.py:210
  161.2 2.2 collective-permute-start.7
  163.4 3.6 %collective-permute-start.6 = (bf16[128,512]{1,0:T(8,128)(2,1)S(1)}, bf16[128,512]{1,0:T(8,128)(2,1)S(1)}, u32[]{:S(2)}, u32[]{:S(2)}) collective-permute-start(bf16[128,512]{1,0:T(8,128)(2,1)S(1)} %fusion.2), channel_id=1, source_target_pairs={{0,32},{16,48},{32,0},{48,16},{1,33},{17,49},{33,1},{49,17},{2,34}... | collective-permute-start | bytes 393224 | tf_op jit(solution)/shard_map/ppermute | solution.py:212
  167.0 2.8 %collective-permute-start.8 = (bf16[128,512]{1,0:T(8,128)(2,1)S(1)}, bf16[128,512]{1,0:T(8,128)(2,1)S(1)}, u32[]{:S(2)}, u32[]{:S(2)}) collective-permute-start(bf16[128,512]{1,0:T(8,128)(2,1)S(1)} %fusion.2), channel_id=1, source_target_pairs={{0,48},{16,0},{32,16},{48,32},{1,49},{17,1},{33,17},{49,33},{2,50}... | collective-permute-start | bytes 393224 | tf_op jit(solution)/shard_map/ppermute | solution.py:212
  169.8 1.0 collective-permute-done.7
  170.9 2.6 %collective-permute-done.6 = bf16[128,512]{1,0:T(8,128)(2,1)S(1)} collective-permute-done((bf16[128,512]{1,0:T(8,128)(2,1)S(1)}, bf16[128,512]{1,0:T(8,128)(2,1)S(1)}, u32[]{:S(2)}, u32[]{:S(2)}) %collective-permute-start.6) | collective-permute-done | bytes 131104 | tf_op jit(solution)/shard_map/ppermute | solution.py:212
  173.4 1.0 collective-permute-done.8
  174.7 22.2 %all_to_all.47 = bf16[8,128,512]{2,1,0:T(8,128)(2,1)} all-to-all(bf16[8,128,512]{2,1,0:T(8,128)(2,1)S(1)} %broadcast_in_dim.8), channel_id=1, replica_groups=mesh['x'=4,'z_high'=4,'z_low'=2,'grp'=8] {'x','z_low'}, dimensions={0} | all-to-all | bytes 2097152 | tf_op jit(solution)/shard_map/all_to_all | solution.py:217
  196.9 10.5 %shard_map.44 = (f32[256,256]{1,0:T(8,128)}, bf16[1024,256]{1,0:T(8,128)(2,1)}) custom-call(bf16[4,256,512]{2,1,0:T(8,128)(2,1)} %bitcast.20, bf16[1024,2048]{1,0:T(8,128)(2,1)} %keys_hbm.7), custom_call_target="tpu_custom_call" | custom-call | tf_op jit(solution)/shard_map/pallas_call | solution.py:187
  207.4 7.4 %all-to-all-start.6 = ((bf16[32,32,256]{2,1,0:T(8,128)(2,1)}), bf16[32,32,256]{2,1,0:T(8,128)(2,1)S(1)}, u32[]{:S(2)}, u32[]{:S(2)}) async-start(bf16[32,32,256]{2,1,0:T(8,128)(2,1)} %bitcast.28), calls=%async_computation.6 | async-start | bytes 1048576 | tf_op jit(solution)/shard_map/all_to_all | solution.py:242
  214.8 3.4 %shard_map.45 = f32[2048,256]{1,0:T(8,128)} custom-call(bf16[4,256,512]{2,1,0:T(8,128)(2,1)} %bitcast.21, f32[256,256]{1,0:T(8,128)} %get-tuple-element.4.inv), custom_call_target="tpu_custom_call" | custom-call | flops 536870912 | bytes 4194304 | tf_op jit(solution)/shard_map/pallas_call | solution.py:187
  218.3 13.3 %all-to-all-done.6 = bf16[32,32,256]{2,1,0:T(8,128)(2,1)S(1)} async-done(((bf16[32,32,256]{2,1,0:T(8,128)(2,1)}), bf16[32,32,256]{2,1,0:T(8,128)(2,1)S(1)}, u32[]{:S(2)}, u32[]{:S(2)}) %all-to-all-start.6) | async-done | bytes 524320 | tf_op jit(solution)/shard_map/all_to_all | solution.py:242
  231.5 0.8 copy.5
  (9 shorter events, 1.0 us)
Async XLA Ops:
  26.8 10.7 %collective-permute-start.1 = (bf16[128,512]{1,0:T(8,128)(2,1)S(1)}, bf16[128,512]{1,0:T(8,128)(2,1)S(1)}, u32[]{:S(2)}, u32[]{:S(2)}) collective-permute-start(bf16[128,512]{1,0:T(8,128)(2,1)S(1)} %fusion), channel_id=1, source_target_pairs={{0,16},{16,32},{32,48},{48,0},{1,17},{17,33},{33,49},{49,1},{2,18}... | collective-permute-start | bytes 393224 | tf_op jit(solution)/shard_map/ppermute | solution.py:212
  30.2 11.8 %collective-permute-start = (bf16[128,512]{1,0:T(8,128)(2,1)S(1)}, bf16[128,512]{1,0:T(8,128)(2,1)S(1)}, u32[]{:S(2)}, u32[]{:S(2)}) collective-permute-start(bf16[128,512]{1,0:T(8,128)(2,1)S(1)} %fusion), channel_id=1, source_target_pairs={{0,32},{16,48},{32,0},{48,16},{1,33},{17,49},{33,1},{49,17},{2,34}... | collective-permute-start | bytes 393224 | tf_op jit(solution)/shard_map/ppermute | solution.py:212
  34.6 8.3 %collective-permute-start.2 = (bf16[128,512]{1,0:T(8,128)(2,1)S(1)}, bf16[128,512]{1,0:T(8,128)(2,1)S(1)}, u32[]{:S(2)}, u32[]{:S(2)}) collective-permute-start(bf16[128,512]{1,0:T(8,128)(2,1)S(1)} %fusion), channel_id=1, source_target_pairs={{0,48},{16,0},{32,16},{48,32},{1,49},{17,1},{33,17},{49,33},{2,50}... | collective-permute-start | bytes 393224 | tf_op jit(solution)/shard_map/ppermute | solution.py:212
  95.1 8.9 %collective-permute-start.4 = (bf16[128,512]{1,0:T(8,128)(2,1)S(1)}, bf16[128,512]{1,0:T(8,128)(2,1)S(1)}, u32[]{:S(2)}, u32[]{:S(2)}) collective-permute-start(bf16[128,512]{1,0:T(8,128)(2,1)S(1)} %fusion.1), channel_id=1, source_target_pairs={{0,16},{16,32},{32,48},{48,0},{1,17},{17,33},{33,49},{49,1},{2,18}... | collective-permute-start | bytes 393224 | tf_op jit(solution)/shard_map/ppermute | solution.py:212
  97.4 9.7 %collective-permute-start.3 = (bf16[128,512]{1,0:T(8,128)(2,1)S(1)}, bf16[128,512]{1,0:T(8,128)(2,1)S(1)}, u32[]{:S(2)}, u32[]{:S(2)}) collective-permute-start(bf16[128,512]{1,0:T(8,128)(2,1)S(1)} %fusion.1), channel_id=1, source_target_pairs={{0,32},{16,48},{32,0},{48,16},{1,33},{17,49},{33,1},{49,17},{2,34}... | collective-permute-start | bytes 393224 | tf_op jit(solution)/shard_map/ppermute | solution.py:212
  101.1 7.2 %collective-permute-start.5 = (bf16[128,512]{1,0:T(8,128)(2,1)S(1)}, bf16[128,512]{1,0:T(8,128)(2,1)S(1)}, u32[]{:S(2)}, u32[]{:S(2)}) collective-permute-start(bf16[128,512]{1,0:T(8,128)(2,1)S(1)} %fusion.1), channel_id=1, source_target_pairs={{0,48},{16,0},{32,16},{48,32},{1,49},{17,1},{33,17},{49,33},{2,50}... | collective-permute-start | bytes 393224 | tf_op jit(solution)/shard_map/ppermute | solution.py:212
  161.2 9.6 %collective-permute-start.7 = (bf16[128,512]{1,0:T(8,128)(2,1)S(1)}, bf16[128,512]{1,0:T(8,128)(2,1)S(1)}, u32[]{:S(2)}, u32[]{:S(2)}) collective-permute-start(bf16[128,512]{1,0:T(8,128)(2,1)S(1)} %fusion.2), channel_id=1, source_target_pairs={{0,16},{16,32},{32,48},{48,0},{1,17},{17,33},{33,49},{49,1},{2,18}... | collective-permute-start | bytes 393224 | tf_op jit(solution)/shard_map/ppermute | solution.py:212
  163.4 10.0 %collective-permute-start.6 = (bf16[128,512]{1,0:T(8,128)(2,1)S(1)}, bf16[128,512]{1,0:T(8,128)(2,1)S(1)}, u32[]{:S(2)}, u32[]{:S(2)}) collective-permute-start(bf16[128,512]{1,0:T(8,128)(2,1)S(1)} %fusion.2), channel_id=1, source_target_pairs={{0,32},{16,48},{32,0},{48,16},{1,33},{17,49},{33,1},{49,17},{2,34}... | collective-permute-start | bytes 393224 | tf_op jit(solution)/shard_map/ppermute | solution.py:212
  167.0 7.4 %collective-permute-start.8 = (bf16[128,512]{1,0:T(8,128)(2,1)S(1)}, bf16[128,512]{1,0:T(8,128)(2,1)S(1)}, u32[]{:S(2)}, u32[]{:S(2)}) collective-permute-start(bf16[128,512]{1,0:T(8,128)(2,1)S(1)} %fusion.2), channel_id=1, source_target_pairs={{0,48},{16,0},{32,16},{48,32},{1,49},{17,1},{33,17},{49,33},{2,50}... | collective-permute-start | bytes 393224 | tf_op jit(solution)/shard_map/ppermute | solution.py:212
  207.4 24.1 %all-to-all-start.6 = ((bf16[32,32,256]{2,1,0:T(8,128)(2,1)}), bf16[32,32,256]{2,1,0:T(8,128)(2,1)S(1)}, u32[]{:S(2)}, u32[]{:S(2)}) async-start(bf16[32,32,256]{2,1,0:T(8,128)(2,1)} %bitcast.28), calls=%async_computation.6 | async-start | bytes 1048576 | tf_op jit(solution)/shard_map/all_to_all | solution.py:242

commit v4 on v3

--- a/solution.py
+++ b/solution.py
@@ -12,9 +12,17 @@
 NZ_LOW = 2
 NB = 32
 GROUP = 8
+CHUNKS = 4
 STRIP = 16
+NZ = NZ_HIGH * NZ_LOW
 AXES = ("x", "z_high", "z_low", "grp")
-VMEM_BYTES = 59_500_000
+POS = AXES[:3]
+NEAR = [
+    [x * NZ + 2 * high + (low ^ (high % 2)) for x in range(NX) for low in range(NZ_LOW)]
+    for high in range(NZ_HIGH)
+]
+PAIRS = (((1, 2), (3, 4), (5, 6), (7, 0)), ((0, 3), (2, 5), (4, 7), (6, 1)))
+VMEM_BYTES = 54_000_000
 F32 = jnp.float32
 BF16 = jnp.bfloat16
 
@@ -84,7 +92,7 @@
     return rows, inverse
 
 
-def inverse_factor(gram, inv):
+def inverse_factor(gram, inv, beside):
     n = gram.shape[0]
     eye = lax.broadcasted_iota(jnp.int32, (n, n), 0) == lax.broadcasted_iota(jnp.int32, (n, n), 1)
     inv[...] = eye.astype(F32)
@@ -93,6 +101,7 @@
         left = start // 128 * 128
         right = -(-done // 128) * 128
         groups = [pl.ds(start + g, GROUP) for g in range(0, NB, GROUP)]
+        beside(start // NB)
         upper, lower = eliminate(
             [gram[g, left:] for g in groups], [inv[g, :right] for g in groups], start - left
         )
@@ -109,16 +118,6 @@
             inv[rest, :right] = inv[rest, :right] - update[done - keep :]
 
 
-def products(keys, basis, out):
-    width = basis[0].shape[1]
-    projected = 0.0
-    for x in range(NX):
-        projected = projected + dot(basis[x], keys[:, x * width : (x + 1) * width], NT)
-    projected = projected.astype(BF16)
-    for x in range(NX):
-        out[x] = dot(projected, keys[:, x * width : (x + 1) * width], NN).astype(BF16)
-
-
 def first_kernel(keys_hbm, basis_hbm, out, keys, basis, key_sems, basis_sems):
     width = keys.shape[1] // NX
     copies = []
@@ -145,34 +144,68 @@
     return [dot(high, summed[x], NN) + dot(mid, summed[x], NN) for x in range(NX)]
 
 
-def factorize(summed, gram, inv):
+def factorize(summed, gram, inv, multiply):
     total = 0.0
     for x in range(NX):
         total = total + dot(summed[x], summed[x], NT)
     gram[...] = total
-    inverse_factor(gram, inv)
-
-
-def middle_kernel(summed, keys_hbm, out, gram, inv, keys, sem):
+    blocks = gram.shape[0] // NB
+
+    def beside(block):
+        if block >= blocks - CHUNKS:
+            multiply(block - (blocks - CHUNKS))
+
+    inverse_factor(gram, inv, beside)
+
+
+def two_part(a):
+    high, mid, _ = split(a)
+    return high, mid
+
+
+def three_products(a, b, dims):
+    (a_high, a_mid), (b_high, b_mid) = two_part(a), two_part(b)
+    return dot(a_high, b_high, dims) + dot(a_high, b_mid, dims) + dot(a_mid, b_high, dims)
+
+
+def middle_kernel(summed, keys_hbm, out, gram, inv, mixed, keys, sem):
     copy = pltpu.make_async_copy(keys_hbm, keys, sem)
     copy.start()
-    factorize(summed, gram, inv)
-    basis = [b.astype(BF16) for b in basis_blocks(summed, inv[...])]
-    copy.wait()
-    products(keys, basis, out)
-
-
-def last_kernel(summed, keys_hbm, inv, out, gram, keys, sem):
+    width = summed.shape[2]
+    size = keys.shape[0] // CHUNKS
+
+    def multiply(chunk):
+        if chunk == 0:
+            copy.wait()
+        at = chunk * size
+        total = 0.0
+        for x in range(NX):
+            total = total + dot(summed[x], keys[at : at + size, x * width : (x + 1) * width], NT)
+        mixed[:, at : at + size] = total
+
+    factorize(summed, gram, inv, multiply)
+    projected = three_products(inv[...], mixed[...], NN).astype(BF16)
+    for x in range(NX):
+        out[x] = dot(projected, keys[:, x * width : (x + 1) * width], NN).astype(BF16)
+
+
+def last_kernel(summed, keys_hbm, inv, out, gram, mixed, keys, sem):
     copy = pltpu.make_async_copy(keys_hbm, keys, sem)
     copy.start()
-    factorize(summed, gram, inv)
     width = summed.shape[2]
-    basis = [b.astype(BF16) for b in basis_blocks(summed, inv[...])]
-    copy.wait()
-    compressed = 0.0
-    for x in range(NX):
-        compressed = compressed + dot(keys[:, x * width : (x + 1) * width], basis[x], NT)
-    out[...] = compressed.astype(BF16)
+    size = keys.shape[0] // CHUNKS
+
+    def multiply(chunk):
+        if chunk == 0:
+            copy.wait()
+        at = chunk * size
+        total = 0.0
+        for x in range(NX):
+            total = total + dot(keys[at : at + size, x * width : (x + 1) * width], summed[x], NT)
+        mixed[at : at + size, :] = total
+
+    factorize(summed, gram, inv, multiply)
+    out[...] = three_products(mixed[...], inv[...], NT).astype(BF16)
 
 
 def basis_kernel(summed, inv, out):
@@ -183,7 +216,7 @@
 
 
 def call(body, out_shape, operands, in_hbm, scratch, cost=None):
-    spec = [pl.BlockSpec(memory_space=pl.ANY if h else pltpu.VMEM) for h in in_hbm]
+    spec = [pl.BlockSpec(memory_space=pltpu.HBM if h else pltpu.VMEM) for h in in_hbm]
     return pl.pallas_call(
         body,
         out_shape=out_shape,
@@ -207,14 +240,15 @@
     near = NX * NZ_LOW
     part = rank // NZ_LOW
     terms = local_term.reshape(near, part, width)
-    own = add_up(lax.all_to_all(terms, ("x", "z_low"), 0, 0, tiled=True))
-    first, second, third = (
-        lax.ppermute(own, "z_high", [(i, (i + step) % NZ_HIGH) for i in range(NZ_HIGH)]).astype(F32)
-        for step in range(1, NZ_HIGH)
-    )
-    total = ((own.astype(F32) + second) + (first + third)).astype(BF16)
+    own = add_up(lax.all_to_all(terms, POS, 0, 0, axis_index_groups=NEAR, tiled=True))
+    for pairs in PAIRS:
+        both_ways = [
+            (x * NZ + p, x * NZ + q) for x in range(NX) for a, b in pairs for p, q in ((a, b), (b, a))
+        ]
+        own = (own.astype(F32) + lax.ppermute(own, POS, both_ways).astype(F32)).astype(BF16)
+    total = own
     total = jnp.broadcast_to(total[None], (near, part, width))
-    blocks = lax.all_to_all(total, ("x", "z_low"), 0, 0, tiled=True)
+    blocks = lax.all_to_all(total, POS, 0, 0, axis_index_groups=NEAR, tiled=True)
     return blocks.reshape(NX, rank, width)
 
 
@@ -232,13 +266,12 @@
     term = call(first_kernel, blocks, (key_cache, init_basis), (True, True), scratch)
     for sweep in range(ITERS - 1):
         summed = sum_and_spread(term)
-        scratch = [square, square, keys, sem]
+        scratch = [square, square, pltpu.VMEM((rank, positions), F32), keys, sem]
         term = call(middle_kernel, blocks, (summed, key_cache), (False, True), scratch)
     summed = sum_and_spread(term)
     outs = (shape((rank, rank), F32), shape((positions, rank), BF16))
-    inv, compressed = call(
-        last_kernel, outs, (summed, key_cache), (False, True), [square, keys, sem]
-    )
+    scratch = [square, pltpu.VMEM((positions, rank), F32), keys, sem]
+    inv, compressed = call(last_kernel, outs, (summed, key_cache), (False, True), scratch)
     latents = lax.all_to_all(
         compressed, ("x", "z_high", "z_low"), split_axis=0, concat_axis=0, tiled=True
     )

time: 233 us -> 197 us (0.85)
  blocking collectives: 123 us -> 96.9 us
  Pallas kernels: 43.3 us -> 32.4 us
  waiting for transfers between devices: 27.9 us -> 36.4 us
  starting transfers between devices: 35.4 us -> 28.3 us
    all_to_all x6, blocking collectives: 123 us -> 96.9 us  [the longest x3 48.5 us: sum_and_spread(): lax.all_to_all(total, POS, 0, 0, axis_index_groups=NEAR, tiled=True)]
    pallas_call x5, Pallas kernels: 43.3 us -> 32.4 us  [call(): pl.pallas_call(body, out_shape=out_shape, in_specs=spec, out_specs=jax.tr...]
    ppermute x9 -> x6, waiting for transfers between devices: 14.7 us -> 25.2 us  [sum_and_spread(): lax.ppermute(own, POS, both_ways).astype(F32)]
    ppermute x9 -> x6, starting transfers between devices: 28 us -> 20.3 us  [sum_and_spread(): lax.ppermute(own, POS, both_ways).astype(F32)]
  transfers between devices with their start and end apart: 10 -> 7, of which waited for: 9 -> 7; matrix products, arithmetic and copies ran while one was open for 0% -> 0% of each run, Pallas kernels for 1% -> 1%
where the time goes in v4:
time: 197 us
  blocking collectives  96.9 us (49%)
  waiting for transfers between devices  36.4 us (18%)
  Pallas kernels  32.4 us (16%)
  starting transfers between devices  28.3 us (14%)
    all_to_all x3, blocking collectives, sum_and_spread(): lax.all_to_all(total, POS, 0, 0, axis_index_groups=NEAR, tiled=True)  48.5 us
    all_to_all x3, blocking collectives, sum_and_spread(): lax.all_to_all(terms, POS, 0, 0, axis_index_groups=NEAR, tiled=True)  48.4 us
    pallas_call x5, Pallas kernels, call(): pl.pallas_call(body, out_shape=out_shape, in_specs=spec, out_specs=jax.tr...  32.4 us
    ppermute x6, waiting for transfers between devices, sum_and_spread(): lax.ppermute(own, POS, both_ways).astype(F32)  25.2 us
    ppermute x6, starting transfers between devices, sum_and_spread(): lax.ppermute(own, POS, both_ways).astype(F32)  20.3 us
    all_to_all x1, waiting for transfers between devices, local(): lax.all_to_all(compressed, ('x', 'z_high', 'z_low'), split_axis=0, concat...  11.3 us
    all_to_all x1, starting transfers between devices, local(): lax.all_to_all(compressed, ('x', 'z_high', 'z_low'), split_axis=0, concat...  7.94 us
  transfers between devices with their start and end apart: 7, of which 7 were waited for; matrix products, arithmetic and copies ran while one was open for 0% of the time, Pallas kernels for 1%

profile of v4, /device:TPU:56, one launch (start us, length us, event | category | flops | bytes accessed | tf_op | source)
XLA Modules:
  0.0 196.8 jit_solution(17187623161113294344)
XLA Ops:
  0.6 4.8 %shard_map.41 = bf16[4,256,512]{2,1,0:T(8,128)(2,1)S(1)} custom-call(bf16[1024,2048]{1,0:T(8,128)(2,1)} %keys_hbm.7, f32[2048,256]{1,0:T(8,128)} %basis_hbm.1), custom_call_target="tpu_custom_call" | custom-call | tf_op jit(solution)/shard_map/pallas_call | solution.py:220
  5.4 20.1 %all_to_all.42 = bf16[8,128,512]{2,1,0:T(8,128)(2,1)S(1)} all-to-all(bf16[8,128,512]{2,1,0:T(8,128)(2,1)S(1)} %bitcast.22), channel_id=1, replica_groups={{0,8,64,72,128,136,192,200},{24,16,88,80,152,144,216,208},{32,40,96,104..., dimensions={0} | all-to-all | bytes 2097152 | tf_op jit(solution)/shard_map/all_to_all | solution.py:243
  25.5 0.1 fusion
  25.6 2.5 %collective-permute-start = (bf16[128,512]{1,0:T(8,128)(2,1)S(1)}, bf16[128,512]{1,0:T(8,128)(2,1)S(1)}, u32[]{:S(2)}, u32[]{:S(2)}) collective-permute-start(bf16[128,512]{1,0:T(8,128)(2,1)S(1)} %fusion), channel_id=1, source_target_pairs={{8,16},{16,8},{24,32},{32,24},{40,48},{48,40},{56,0},{0,56},{72,80... | collective-permute-start | bytes 393224 | tf_op jit(solution)/shard_map/ppermute | solution.py:248
  28.1 2.9 %collective-permute-done = bf16[128,512]{1,0:T(8,128)(2,1)S(1)} collective-permute-done((bf16[128,512]{1,0:T(8,128)(2,1)S(1)}, bf16[128,512]{1,0:T(8,128)(2,1)S(1)}, u32[]{:S(2)}, u32[]{:S(2)}) %collective-permute-start) | collective-permute-done | bytes 131104 | tf_op jit(solution)/shard_map/ppermute | solution.py:248
  31.0 0.2 add_convert_fusion.7
  31.2 5.6 %collective-permute-start.1 = (bf16[128,512]{1,0:T(8,128)(2,1)S(1)}, bf16[128,512]{1,0:T(8,128)(2,1)S(1)}, u32[]{:S(2)}, u32[]{:S(2)}) collective-permute-start(bf16[128,512]{1,0:T(8,128)(2,1)S(1)} %add_convert_fusion.7), channel_id=1, source_target_pairs={{0,24},{24,0},{16,40},{40,16},{32,56},{56,32},{48,8},{8,48},{64,88... | collective-permute-start | bytes 393224 | tf_op jit(solution)/shard_map/ppermute | solution.py:248
  36.8 3.7 %collective-permute-done.1 = bf16[128,512]{1,0:T(8,128)(2,1)S(1)} collective-permute-done((bf16[128,512]{1,0:T(8,128)(2,1)S(1)}, bf16[128,512]{1,0:T(8,128)(2,1)S(1)}, u32[]{:S(2)}, u32[]{:S(2)}) %collective-permute-start.1) | collective-permute-done | bytes 131104 | tf_op jit(solution)/shard_map/ppermute | solution.py:248
  40.6 16.8 %all_to_all.43 = bf16[8,128,512]{2,1,0:T(8,128)(2,1)S(1)} all-to-all(bf16[8,128,512]{2,1,0:T(8,128)(2,1)S(1)} %broadcast_in_dim.6), channel_id=1, replica_groups={{0,8,64,72,128,136,192,200},{24,16,88,80,152,144,216,208},{32,40,96,104..., dimensions={0} | all-to-all | bytes 2097152 | tf_op jit(solution)/shard_map/all_to_all | solution.py:251
  57.4 8.6 %shard_map.42 = bf16[4,256,512]{2,1,0:T(8,128)(2,1)S(1)} custom-call(bf16[4,256,512]{2,1,0:T(8,128)(2,1)S(1)} %bitcast.23, bf16[1024,2048]{1,0:T(8,128)(2,1)} %keys_hbm.7), custom_call_target="tpu_custom_call" | custom-call | tf_op jit(solution)/shard_map/pallas_call | solution.py:220
  66.1 14.3 %all_to_all.44 = bf16[8,128,512]{2,1,0:T(8,128)(2,1)S(1)} all-to-all(bf16[8,128,512]{2,1,0:T(8,128)(2,1)S(1)} %bitcast.24), channel_id=1, replica_groups={{0,8,64,72,128,136,192,200},{24,16,88,80,152,144,216,208},{32,40,96,104..., dimensions={0} | all-to-all | bytes 2097152 | tf_op jit(solution)/shard_map/all_to_all | solution.py:243
  80.4 0.1 fusion.1
  80.5 1.1 collective-permute-start.2
  81.6 5.0 %collective-permute-done.2 = bf16[128,512]{1,0:T(8,128)(2,1)S(1)} collective-permute-done((bf16[128,512]{1,0:T(8,128)(2,1)S(1)}, bf16[128,512]{1,0:T(8,128)(2,1)S(1)}, u32[]{:S(2)}, u32[]{:S(2)}) %collective-permute-start.2) | collective-permute-done | bytes 131104 | tf_op jit(solution)/shard_map/ppermute | solution.py:248
  86.6 0.2 add_convert_fusion.4
  86.8 4.5 %collective-permute-start.3 = (bf16[128,512]{1,0:T(8,128)(2,1)S(1)}, bf16[128,512]{1,0:T(8,128)(2,1)S(1)}, u32[]{:S(2)}, u32[]{:S(2)}) collective-permute-start(bf16[128,512]{1,0:T(8,128)(2,1)S(1)} %add_convert_fusion.4), channel_id=1, source_target_pairs={{0,24},{24,0},{16,40},{40,16},{32,56},{56,32},{48,8},{8,48},{64,88... | collective-permute-start | bytes 393224 | tf_op jit(solution)/shard_map/ppermute | solution.py:248
  91.3 4.8 %collective-permute-done.3 = bf16[128,512]{1,0:T(8,128)(2,1)S(1)} collective-permute-done((bf16[128,512]{1,0:T(8,128)(2,1)S(1)}, bf16[128,512]{1,0:T(8,128)(2,1)S(1)}, u32[]{:S(2)}, u32[]{:S(2)}) %collective-permute-start.3) | collective-permute-done | bytes 131104 | tf_op jit(solution)/shard_map/ppermute | solution.py:248
  96.2 15.2 %all_to_all.45 = bf16[8,128,512]{2,1,0:T(8,128)(2,1)S(1)} all-to-all(bf16[8,128,512]{2,1,0:T(8,128)(2,1)S(1)} %broadcast_in_dim.7), channel_id=1, replica_groups={{0,8,64,72,128,136,192,200},{24,16,88,80,152,144,216,208},{32,40,96,104..., dimensions={0} | all-to-all | bytes 2097152 | tf_op jit(solution)/shard_map/all_to_all | solution.py:251
  111.4 8.6 %shard_map.43 = bf16[4,256,512]{2,1,0:T(8,128)(2,1)S(1)} custom-call(bf16[4,256,512]{2,1,0:T(8,128)(2,1)S(1)} %bitcast.25, bf16[1024,2048]{1,0:T(8,128)(2,1)} %keys_hbm.7), custom_call_target="tpu_custom_call" | custom-call | tf_op jit(solution)/shard_map/pallas_call | solution.py:220
  120.0 14.0 %all_to_all.46 = bf16[8,128,512]{2,1,0:T(8,128)(2,1)S(1)} all-to-all(bf16[8,128,512]{2,1,0:T(8,128)(2,1)S(1)} %bitcast.26), channel_id=1, replica_groups={{0,8,64,72,128,136,192,200},{24,16,88,80,152,144,216,208},{32,40,96,104..., dimensions={0} | all-to-all | bytes 2097152 | tf_op jit(solution)/shard_map/all_to_all | solution.py:243
  134.1 0.1 fusion.2
  134.2 0.8 collective-permute-start.4
  135.0 4.3 %collective-permute-done.4 = bf16[128,512]{1,0:T(8,128)(2,1)S(1)} collective-permute-done((bf16[128,512]{1,0:T(8,128)(2,1)S(1)}, bf16[128,512]{1,0:T(8,128)(2,1)S(1)}, u32[]{:S(2)}, u32[]{:S(2)}) %collective-permute-start.4) | collective-permute-done | bytes 131104 | tf_op jit(solution)/shard_map/ppermute | solution.py:248
  139.2 0.2 add_convert_fusion.1
  139.4 5.9 %collective-permute-start.5 = (bf16[128,512]{1,0:T(8,128)(2,1)S(1)}, bf16[128,512]{1,0:T(8,128)(2,1)S(1)}, u32[]{:S(2)}, u32[]{:S(2)}) collective-permute-start(bf16[128,512]{1,0:T(8,128)(2,1)S(1)} %add_convert_fusion.1), channel_id=1, source_target_pairs={{0,24},{24,0},{16,40},{40,16},{32,56},{56,32},{48,8},{8,48},{64,88... | collective-permute-start | bytes 393224 | tf_op jit(solution)/shard_map/ppermute | solution.py:248
  145.3 4.4 %collective-permute-done.5 = bf16[128,512]{1,0:T(8,128)(2,1)S(1)} collective-permute-done((bf16[128,512]{1,0:T(8,128)(2,1)S(1)}, bf16[128,512]{1,0:T(8,128)(2,1)S(1)}, u32[]{:S(2)}, u32[]{:S(2)}) %collective-permute-start.5) | collective-permute-done | bytes 131104 | tf_op jit(solution)/shard_map/ppermute | solution.py:248
  149.8 16.5 %all_to_all.47 = bf16[8,128,512]{2,1,0:T(8,128)(2,1)S(1)} all-to-all(bf16[8,128,512]{2,1,0:T(8,128)(2,1)S(1)} %broadcast_in_dim.8), channel_id=1, replica_groups={{0,8,64,72,128,136,192,200},{24,16,88,80,152,144,216,208},{32,40,96,104..., dimensions={0} | all-to-all | bytes 2097152 | tf_op jit(solution)/shard_map/all_to_all | solution.py:251
  166.4 8.2 %shard_map.44 = (f32[256,256]{1,0:T(8,128)S(1)}, bf16[1024,256]{1,0:T(8,128)(2,1)}) custom-call(bf16[4,256,512]{2,1,0:T(8,128)(2,1)S(1)} %bitcast.20, bf16[1024,2048]{1,0:T(8,128)(2,1)} %keys_hbm.7), custom_call_target="tpu_custom_call" | custom-call | tf_op jit(solution)/shard_map/pallas_call | solution.py:220
  174.6 7.9 %all-to-all-start.6 = ((bf16[32,32,256]{2,1,0:T(8,128)(2,1)}), bf16[32,32,256]{2,1,0:T(8,128)(2,1)S(1)}, u32[]{:S(2)}, u32[]{:S(2)}) async-start(bf16[32,32,256]{2,1,0:T(8,128)(2,1)} %bitcast.9), calls=%async_computation.6 | async-start | bytes 1048576 | tf_op jit(solution)/shard_map/all_to_all | solution.py:275
  182.6 2.2 %shard_map.45 = f32[2048,256]{1,0:T(8,128)} custom-call(bf16[4,256,512]{2,1,0:T(8,128)(2,1)S(1)} %bitcast.21, f32[256,256]{1,0:T(8,128)S(1)} %get-tuple-element.4.inv), custom_call_target="tpu_custom_call" | custom-call | flops 536870912 | bytes 4194304 | tf_op jit(solution)/shard_map/pallas_call | solution.py:220
  184.7 11.3 %all-to-all-done.6 = bf16[32,32,256]{2,1,0:T(8,128)(2,1)S(1)} async-done(((bf16[32,32,256]{2,1,0:T(8,128)(2,1)}), bf16[32,32,256]{2,1,0:T(8,128)(2,1)S(1)}, u32[]{:S(2)}, u32[]{:S(2)}) %all-to-all-start.6) | async-done | bytes 524320 | tf_op jit(solution)/shard_map/all_to_all | solution.py:275
  196.0 0.8 copy.5
  (6 shorter events, 0.3 us)
Async XLA Ops:
  25.6 5.4 %collective-permute-start = (bf16[128,512]{1,0:T(8,128)(2,1)S(1)}, bf16[128,512]{1,0:T(8,128)(2,1)S(1)}, u32[]{:S(2)}, u32[]{:S(2)}) collective-permute-start(bf16[128,512]{1,0:T(8,128)(2,1)S(1)} %fusion), channel_id=1, source_target_pairs={{8,16},{16,8},{24,32},{32,24},{40,48},{48,40},{56,0},{0,56},{72,80... | collective-permute-start | bytes 393224 | tf_op jit(solution)/shard_map/ppermute | solution.py:248
  31.2 9.3 %collective-permute-start.1 = (bf16[128,512]{1,0:T(8,128)(2,1)S(1)}, bf16[128,512]{1,0:T(8,128)(2,1)S(1)}, u32[]{:S(2)}, u32[]{:S(2)}) collective-permute-start(bf16[128,512]{1,0:T(8,128)(2,1)S(1)} %add_convert_fusion.7), channel_id=1, source_target_pairs={{0,24},{24,0},{16,40},{40,16},{32,56},{56,32},{48,8},{8,48},{64,88... | collective-permute-start | bytes 393224 | tf_op jit(solution)/shard_map/ppermute | solution.py:248
  80.5 6.1 %collective-permute-start.2 = (bf16[128,512]{1,0:T(8,128)(2,1)S(1)}, bf16[128,512]{1,0:T(8,128)(2,1)S(1)}, u32[]{:S(2)}, u32[]{:S(2)}) collective-permute-start(bf16[128,512]{1,0:T(8,128)(2,1)S(1)} %fusion.1), channel_id=1, source_target_pairs={{8,16},{16,8},{24,32},{32,24},{40,48},{48,40},{56,0},{0,56},{72,80... | collective-permute-start | bytes 393224 | tf_op jit(solution)/shard_map/ppermute | solution.py:248
  86.8 9.3 %collective-permute-start.3 = (bf16[128,512]{1,0:T(8,128)(2,1)S(1)}, bf16[128,512]{1,0:T(8,128)(2,1)S(1)}, u32[]{:S(2)}, u32[]{:S(2)}) collective-permute-start(bf16[128,512]{1,0:T(8,128)(2,1)S(1)} %add_convert_fusion.4), channel_id=1, source_target_pairs={{0,24},{24,0},{16,40},{40,16},{32,56},{56,32},{48,8},{8,48},{64,88... | collective-permute-start | bytes 393224 | tf_op jit(solution)/shard_map/ppermute | solution.py:248
  134.2 5.1 %collective-permute-start.4 = (bf16[128,512]{1,0:T(8,128)(2,1)S(1)}, bf16[128,512]{1,0:T(8,128)(2,1)S(1)}, u32[]{:S(2)}, u32[]{:S(2)}) collective-permute-start(bf16[128,512]{1,0:T(8,128)(2,1)S(1)} %fusion.2), channel_id=1, source_target_pairs={{8,16},{16,8},{24,32},{32,24},{40,48},{48,40},{56,0},{0,56},{72,80... | collective-permute-start | bytes 393224 | tf_op jit(solution)/shard_map/ppermute | solution.py:248
  139.4 10.3 %collective-permute-start.5 = (bf16[128,512]{1,0:T(8,128)(2,1)S(1)}, bf16[128,512]{1,0:T(8,128)(2,1)S(1)}, u32[]{:S(2)}, u32[]{:S(2)}) collective-permute-start(bf16[128,512]{1,0:T(8,128)(2,1)S(1)} %add_convert_fusion.1), channel_id=1, source_target_pairs={{0,24},{24,0},{16,40},{40,16},{32,56},{56,32},{48,8},{8,48},{64,88... | collective-permute-start | bytes 393224 | tf_op jit(solution)/shard_map/ppermute | solution.py:248
  174.6 21.4 %all-to-all-start.6 = ((bf16[32,32,256]{2,1,0:T(8,128)(2,1)}), bf16[32,32,256]{2,1,0:T(8,128)(2,1)S(1)}, u32[]{:S(2)}, u32[]{:S(2)}) async-start(bf16[32,32,256]{2,1,0:T(8,128)(2,1)} %bitcast.9), calls=%async_computation.6 | async-start | bytes 1048576 | tf_op jit(solution)/shard_map/all_to_all | solution.py:275

commit v5 on v4

--- a/solution.py
+++ b/solution.py
@@ -21,10 +21,14 @@
     [x * NZ + 2 * high + (low ^ (high % 2)) for x in range(NX) for low in range(NZ_LOW)]
     for high in range(NZ_HIGH)
 ]
-PAIRS = (((1, 2), (3, 4), (5, 6), (7, 0)), ((0, 3), (2, 5), (4, 7), (6, 1)))
+PAIRS = (((0, 3), (2, 5), (4, 7), (6, 1)), ((1, 2), (3, 4), (5, 6), (7, 0)))
 VMEM_BYTES = 54_000_000
 F32 = jnp.float32
 BF16 = jnp.bfloat16
+
+TERMS = BF16
+SUMS = F32
+PARTS = 2
 
 NN = (((1,), (0,)), ((), ()))
 NT = (((1,), (1,)), ((), ()))
@@ -136,7 +140,7 @@
         projected = projected + dot(rounded, keys[:, x * width : (x + 1) * width], NT)
     projected = projected.astype(BF16)
     for x in range(NX):
-        out[x] = dot(projected, keys[:, x * width : (x + 1) * width], NN).astype(BF16)
+        out[x] = dot(projected, keys[:, x * width : (x + 1) * width], NN).astype(out.dtype)
 
 
 def basis_blocks(summed, inv):
@@ -168,25 +172,30 @@
     return dot(a_high, b_high, dims) + dot(a_high, b_mid, dims) + dot(a_mid, b_high, dims)
 
 
-def middle_kernel(summed, keys_hbm, out, gram, inv, mixed, keys, sem):
+def middle_kernel(blocks, keys_hbm, out, gram, inv, mixed, keys, sem):
     copy = pltpu.make_async_copy(keys_hbm, keys, sem)
     copy.start()
-    width = summed.shape[2]
+    width = blocks.shape[4]
     size = keys.shape[0] // CHUNKS
+    parts = [
+        [jnp.concatenate([blocks[x, z, p] for z in range(NZ_LOW)], axis=0) for x in range(NX)]
+        for p in range(blocks.shape[2])
+    ]
 
     def multiply(chunk):
         if chunk == 0:
             copy.wait()
         at = chunk * size
         total = 0.0
-        for x in range(NX):
-            total = total + dot(summed[x], keys[at : at + size, x * width : (x + 1) * width], NT)
+        for part in parts:
+            for x in range(NX):
+                total = total + dot(part[x], keys[at : at + size, x * width : (x + 1) * width], NT)
         mixed[:, at : at + size] = total
 
-    factorize(summed, gram, inv, multiply)
+    factorize(parts[0], gram, inv, multiply)
     projected = three_products(inv[...], mixed[...], NN).astype(BF16)
     for x in range(NX):
-        out[x] = dot(projected, keys[:, x * width : (x + 1) * width], NN).astype(BF16)
+        out[x] = dot(projected, keys[:, x * width : (x + 1) * width], NN).astype(out.dtype)
 
 
 def last_kernel(summed, keys_hbm, inv, out, gram, mixed, keys, sem):
@@ -232,24 +241,26 @@
     terms = [terms[i].astype(F32) for i in range(terms.shape[0])]
     while len(terms) > 1:
         terms = [a + b for a, b in zip(terms[0::2], terms[1::2])]
-    return terms[0].astype(BF16)
-
-
-def sum_and_spread(local_term):
+    return terms[0]
+
+
+def sum_and_spread(local_term, sums, parts):
     _, rank, width = local_term.shape
     near = NX * NZ_LOW
     part = rank // NZ_LOW
     terms = local_term.reshape(near, part, width)
-    own = add_up(lax.all_to_all(terms, POS, 0, 0, axis_index_groups=NEAR, tiled=True))
+    terms = lax.all_to_all(terms, POS, 0, 0, axis_index_groups=NEAR, tiled=True)
+    own = add_up(terms).astype(sums)
     for pairs in PAIRS:
         both_ways = [
             (x * NZ + p, x * NZ + q) for x in range(NX) for a, b in pairs for p, q in ((a, b), (b, a))
         ]
-        own = (own.astype(F32) + lax.ppermute(own, POS, both_ways).astype(F32)).astype(BF16)
-    total = own
-    total = jnp.broadcast_to(total[None], (near, part, width))
+        other = lax.ppermute(own, POS, both_ways)
+        own = (own.astype(F32) + other.astype(F32)).astype(sums)
+    total = jnp.stack(split(own.astype(F32))[:parts]) if parts > 1 else own.astype(BF16)[None]
+    total = jnp.broadcast_to(total[None], (near, parts, part, width))
     blocks = lax.all_to_all(total, POS, 0, 0, axis_index_groups=NEAR, tiled=True)
-    return blocks.reshape(NX, rank, width)
+    return blocks.reshape(NX, NZ_LOW, parts, part, width)
 
 
 def local(key_cache, init_basis):
@@ -263,12 +274,12 @@
     blocks = shape((NX, rank, width), BF16)
 
     scratch = [keys, pltpu.VMEM((features, rank), F32), sem((NX,)), sem((NX,))]
-    term = call(first_kernel, blocks, (key_cache, init_basis), (True, True), scratch)
+    term = call(first_kernel, shape((NX, rank, width), TERMS), (key_cache, init_basis), (True, True), scratch)
     for sweep in range(ITERS - 1):
-        summed = sum_and_spread(term)
+        summed = sum_and_spread(term, *((SUMS, PARTS) if sweep == 0 else (BF16, 1)))
         scratch = [square, square, pltpu.VMEM((rank, positions), F32), keys, sem]
         term = call(middle_kernel, blocks, (summed, key_cache), (False, True), scratch)
-    summed = sum_and_spread(term)
+    summed = sum_and_spread(term, BF16, 1).reshape(NX, rank, width)
     outs = (shape((rank, rank), F32), shape((positions, rank), BF16))
     scratch = [square, pltpu.VMEM((positions, rank), F32), keys, sem]
     inv, compressed = call(last_kernel, outs, (summed, key_cache), (False, True), scratch)

time: 197 us -> 215 us (1.091)
  blocking collectives: 96.9 us -> 108 us
  starting transfers between devices: 28.3 us -> 32.2 us
    all_to_all x3, blocking collectives: 48.5 us -> 56.3 us  [sum_and_spread(): lax.all_to_all(total, POS, 0, 0, axis_index_groups=NEAR, tiled=True)]
    ppermute x6, starting transfers between devices: 20.3 us -> 25.2 us  [sum_and_spread(): other = lax.ppermute(own, POS, both_ways)]
    all_to_all x3, blocking collectives: 48.4 us -> 51.2 us  [sum_and_spread(): terms = lax.all_to_all(terms, POS, 0, 0, axis_index_groups=NEAR, tiled=True)]
where the time goes in v5:
time: 215 us
  blocking collectives  108 us (50%)
  waiting for transfers between devices  37.8 us (18%)
  Pallas kernels  34.5 us (16%)
  starting transfers between devices  32.2 us (15%)
    all_to_all x3, blocking collectives, sum_and_spread(): lax.all_to_all(total, POS, 0, 0, axis_index_groups=NEAR, tiled=True)  56.3 us
    all_to_all x3, blocking collectives, sum_and_spread(): terms = lax.all_to_all(terms, POS, 0, 0, axis_index_groups=NEAR, tiled=True)  51.2 us
    pallas_call x5, Pallas kernels, call(): pl.pallas_call(body, out_shape=out_shape, in_specs=spec, out_specs=jax.tr...  34.5 us
    ppermute x6, waiting for transfers between devices, sum_and_spread(): other = lax.ppermute(own, POS, both_ways)  26.6 us
    ppermute x6, starting transfers between devices, sum_and_spread(): other = lax.ppermute(own, POS, both_ways)  25.2 us
    all_to_all x1, waiting for transfers between devices, local(): lax.all_to_all(compressed, ('x', 'z_high', 'z_low'), split_axis=0, concat...  11.3 us
    all_to_all x1, starting transfers between devices, local(): lax.all_to_all(compressed, ('x', 'z_high', 'z_low'), split_axis=0, concat...  6.98 us
  transfers between devices with their start and end apart: 7, of which 7 were waited for; matrix products, arithmetic and copies ran while one was open for 0% of the time, Pallas kernels for 1%

profile of v5, /device:TPU:56, one launch (start us, length us, event | category | flops | bytes accessed | tf_op | source)
XLA Modules:
  0.0 215.0 jit_solution(1763191911522331448)
XLA Ops:
  0.6 4.8 %shard_map.41 = bf16[4,256,512]{2,1,0:T(8,128)(2,1)S(1)} custom-call(bf16[1024,2048]{1,0:T(8,128)(2,1)} %keys_hbm.7, f32[2048,256]{1,0:T(8,128)} %basis_hbm.1), custom_call_target="tpu_custom_call" | custom-call | tf_op jit(solution)/shard_map/pallas_call | solution.py:229
  5.4 20.1 %all_to_all.42 = bf16[8,128,512]{2,1,0:T(8,128)(2,1)S(1)} all-to-all(bf16[8,128,512]{2,1,0:T(8,128)(2,1)S(1)} %bitcast.27), channel_id=1, replica_groups={{0,8,64,72,128,136,192,200},{24,16,88,80,152,144,216,208},{32,40,96,104..., dimensions={0} | all-to-all | bytes 2097152 | tf_op jit(solution)/shard_map/all_to_all | solution.py:252
  25.6 5.9 %collective-permute-start = (f32[128,512]{1,0:T(8,128)S(1)}, f32[128,512]{1,0:T(8,128)S(1)}, u32[]{:S(2)}, u32[]{:S(2)}) collective-permute-start(f32[128,512]{1,0:T(8,128)S(1)} %add_bitcast_fusion), channel_id=1, source_target_pairs={{0,24},{24,0},{16,40},{40,16},{32,56},{56,32},{48,8},{8,48},{64,88... | collective-permute-start | bytes 786440 | tf_op jit(solution)/shard_map/ppermute | solution.py:258
  31.6 7.4 %collective-permute-done = f32[128,512]{1,0:T(8,128)S(1)} collective-permute-done((f32[128,512]{1,0:T(8,128)S(1)}, f32[128,512]{1,0:T(8,128)S(1)}, u32[]{:S(2)}, u32[]{:S(2)}) %collective-permute-start) | collective-permute-done | bytes 262176 | tf_op jit(solution)/shard_map/ppermute | solution.py:258
  39.0 0.1 fusion.4
  39.1 3.8 %collective-permute-start.1 = (f32[128,512]{1,0:T(8,128)S(1)}, f32[128,512]{1,0:T(8,128)S(1)}, u32[]{:S(2)}, u32[]{:S(2)}) collective-permute-start(f32[128,512]{1,0:T(8,128)S(1)} %fusion.4), channel_id=1, source_target_pairs={{8,16},{16,8},{24,32},{32,24},{40,48},{48,40},{56,0},{0,56},{72,80... | collective-permute-start | bytes 786440 | tf_op jit(solution)/shard_map/ppermute | solution.py:258
  43.0 4.4 %collective-permute-done.1 = f32[128,512]{1,0:T(8,128)S(1)} collective-permute-done((f32[128,512]{1,0:T(8,128)S(1)}, f32[128,512]{1,0:T(8,128)S(1)}, u32[]{:S(2)}, u32[]{:S(2)}) %collective-permute-start.1) | collective-permute-done | bytes 262176 | tf_op jit(solution)/shard_map/ppermute | solution.py:258
  47.4 0.2 broadcast_in_dim.6
  47.6 27.3 %all_to_all.43 = bf16[8,2,128,512]{3,2,1,0:T(8,128)(2,1)} all-to-all(bf16[8,2,128,512]{3,2,1,0:T(8,128)(2,1)S(1)} %broadcast_in_dim.6), channel_id=1, replica_groups={{0,8,64,72,128,136,192,200},{24,16,88,80,152,144,216,208},{32,40,96,104..., dimensions={0} | all-to-all | bytes 4194304 | tf_op jit(solution)/shard_map/all_to_all | solution.py:262
  74.9 10.7 %shard_map.42 = bf16[4,256,512]{2,1,0:T(8,128)(2,1)S(1)} custom-call(bf16[4,2,2,128,512]{4,3,2,1,0:T(8,128)(2,1)} %bitcast.30, bf16[1024,2048]{1,0:T(8,128)(2,1)} %keys_hbm.7), custom_call_target="tpu_custom_call" | custom-call | tf_op jit(solution)/shard_map/pallas_call | solution.py:229
  85.6 15.2 %all_to_all.44 = bf16[8,128,512]{2,1,0:T(8,128)(2,1)S(1)} all-to-all(bf16[8,128,512]{2,1,0:T(8,128)(2,1)S(1)} %bitcast.26), channel_id=1, replica_groups={{0,8,64,72,128,136,192,200},{24,16,88,80,152,144,216,208},{32,40,96,104..., dimensions={0} | all-to-all | bytes 2097152 | tf_op jit(solution)/shard_map/all_to_all | solution.py:252
  100.8 0.1 fusion.1
  100.9 5.5 %collective-permute-start.2 = (bf16[128,512]{1,0:T(8,128)(2,1)S(1)}, bf16[128,512]{1,0:T(8,128)(2,1)S(1)}, u32[]{:S(2)}, u32[]{:S(2)}) collective-permute-start(bf16[128,512]{1,0:T(8,128)(2,1)S(1)} %fusion.1), channel_id=1, source_target_pairs={{0,24},{24,0},{16,40},{40,16},{32,56},{56,32},{48,8},{8,48},{64,88... | collective-permute-start | bytes 393224 | tf_op jit(solution)/shard_map/ppermute | solution.py:258
  106.4 3.9 %collective-permute-done.2 = bf16[128,512]{1,0:T(8,128)(2,1)S(1)} collective-permute-done((bf16[128,512]{1,0:T(8,128)(2,1)S(1)}, bf16[128,512]{1,0:T(8,128)(2,1)S(1)}, u32[]{:S(2)}, u32[]{:S(2)}) %collective-permute-start.2) | collective-permute-done | bytes 131104 | tf_op jit(solution)/shard_map/ppermute | solution.py:258
  110.3 0.2 add_convert_fusion.4
  110.5 3.5 %collective-permute-start.3 = (bf16[128,512]{1,0:T(8,128)(2,1)S(1)}, bf16[128,512]{1,0:T(8,128)(2,1)S(1)}, u32[]{:S(2)}, u32[]{:S(2)}) collective-permute-start(bf16[128,512]{1,0:T(8,128)(2,1)S(1)} %add_convert_fusion.4), channel_id=1, source_target_pairs={{8,16},{16,8},{24,32},{32,24},{40,48},{48,40},{56,0},{0,56},{72,80... | collective-permute-start | bytes 393224 | tf_op jit(solution)/shard_map/ppermute | solution.py:258
  114.0 2.9 %collective-permute-done.3 = bf16[128,512]{1,0:T(8,128)(2,1)S(1)} collective-permute-done((bf16[128,512]{1,0:T(8,128)(2,1)S(1)}, bf16[128,512]{1,0:T(8,128)(2,1)S(1)}, u32[]{:S(2)}, u32[]{:S(2)}) %collective-permute-start.3) | collective-permute-done | bytes 131104 | tf_op jit(solution)/shard_map/ppermute | solution.py:258
  117.1 14.3 %all_to_all.45 = bf16[8,1,128,512]{3,2,1,0:T(8,128)(2,1)S(1)} all-to-all(bf16[8,1,128,512]{3,2,1,0:T(8,128)(2,1)S(1)} %broadcast_in_dim.7), channel_id=1, replica_groups={{0,8,64,72,128,136,192,200},{24,16,88,80,152,144,216,208},{32,40,96,104..., dimensions={0} | all-to-all | bytes 2097152 | tf_op jit(solution)/shard_map/all_to_all | solution.py:262
  131.4 8.6 %shard_map.43 = bf16[4,256,512]{2,1,0:T(8,128)(2,1)S(1)} custom-call(bf16[4,2,1,128,512]{4,3,2,1,0:T(8,128)(2,1)S(1)} %bitcast.28, bf16[1024,2048]{1,0:T(8,128)(2,1)} %keys_hbm.7), custom_call_target="tpu_custom_call" | custom-call | tf_op jit(solution)/shard_map/pallas_call | solution.py:229
  140.0 15.9 %all_to_all.46 = bf16[8,128,512]{2,1,0:T(8,128)(2,1)S(1)} all-to-all(bf16[8,128,512]{2,1,0:T(8,128)(2,1)S(1)} %bitcast.29), channel_id=1, replica_groups={{0,8,64,72,128,136,192,200},{24,16,88,80,152,144,216,208},{32,40,96,104..., dimensions={0} | all-to-all | bytes 2097152 | tf_op jit(solution)/shard_map/all_to_all | solution.py:252
  156.0 0.1 fusion.2
  156.1 4.1 %collective-permute-start.4 = (bf16[128,512]{1,0:T(8,128)(2,1)S(1)}, bf16[128,512]{1,0:T(8,128)(2,1)S(1)}, u32[]{:S(2)}, u32[]{:S(2)}) collective-permute-start(bf16[128,512]{1,0:T(8,128)(2,1)S(1)} %fusion.2), channel_id=1, source_target_pairs={{0,24},{24,0},{16,40},{40,16},{32,56},{56,32},{48,8},{8,48},{64,88... | collective-permute-start | bytes 393224 | tf_op jit(solution)/shard_map/ppermute | solution.py:258
  160.2 5.0 %collective-permute-done.4 = bf16[128,512]{1,0:T(8,128)(2,1)S(1)} collective-permute-done((bf16[128,512]{1,0:T(8,128)(2,1)S(1)}, bf16[128,512]{1,0:T(8,128)(2,1)S(1)}, u32[]{:S(2)}, u32[]{:S(2)}) %collective-permute-start.4) | collective-permute-done | bytes 131104 | tf_op jit(solution)/shard_map/ppermute | solution.py:258
  165.3 0.2 add_convert_fusion.1
  165.4 2.2 %collective-permute-start.5 = (bf16[128,512]{1,0:T(8,128)(2,1)S(1)}, bf16[128,512]{1,0:T(8,128)(2,1)S(1)}, u32[]{:S(2)}, u32[]{:S(2)}) collective-permute-start(bf16[128,512]{1,0:T(8,128)(2,1)S(1)} %add_convert_fusion.1), channel_id=1, source_target_pairs={{8,16},{16,8},{24,32},{32,24},{40,48},{48,40},{56,0},{0,56},{72,80... | collective-permute-start | bytes 393224 | tf_op jit(solution)/shard_map/ppermute | solution.py:258
  167.6 2.9 %collective-permute-done.5 = bf16[128,512]{1,0:T(8,128)(2,1)S(1)} collective-permute-done((bf16[128,512]{1,0:T(8,128)(2,1)S(1)}, bf16[128,512]{1,0:T(8,128)(2,1)S(1)}, u32[]{:S(2)}, u32[]{:S(2)}) %collective-permute-start.5) | collective-permute-done | bytes 131104 | tf_op jit(solution)/shard_map/ppermute | solution.py:258
  170.7 14.8 %all_to_all.47 = bf16[8,1,128,512]{3,2,1,0:T(8,128)(2,1)S(1)} all-to-all(bf16[8,1,128,512]{3,2,1,0:T(8,128)(2,1)S(1)} %broadcast_in_dim.8), channel_id=1, replica_groups={{0,8,64,72,128,136,192,200},{24,16,88,80,152,144,216,208},{32,40,96,104..., dimensions={0} | all-to-all | bytes 2097152 | tf_op jit(solution)/shard_map/all_to_all | solution.py:262
  185.5 8.3 %shard_map.44 = (f32[256,256]{1,0:T(8,128)S(1)}, bf16[1024,256]{1,0:T(8,128)(2,1)}) custom-call(bf16[4,256,512]{2,1,0:T(8,128)(2,1)S(1)} %bitcast.24, bf16[1024,2048]{1,0:T(8,128)(2,1)} %keys_hbm.7), custom_call_target="tpu_custom_call" | custom-call | tf_op jit(solution)/shard_map/pallas_call | solution.py:229
  193.8 7.0 %all-to-all-start.6 = ((bf16[32,32,256]{2,1,0:T(8,128)(2,1)}), bf16[32,32,256]{2,1,0:T(8,128)(2,1)S(1)}, u32[]{:S(2)}, u32[]{:S(2)}) async-start(bf16[32,32,256]{2,1,0:T(8,128)(2,1)} %bitcast.11), calls=%async_computation.6 | async-start | bytes 1048576 | tf_op jit(solution)/shard_map/all_to_all | solution.py:286
  200.8 2.2 %shard_map.45 = f32[2048,256]{1,0:T(8,128)} custom-call(bf16[4,256,512]{2,1,0:T(8,128)(2,1)S(1)} %bitcast.25, f32[256,256]{1,0:T(8,128)S(1)} %get-tuple-element.4.inv), custom_call_target="tpu_custom_call" | custom-call | flops 536870912 | bytes 4194304 | tf_op jit(solution)/shard_map/pallas_call | solution.py:229
  202.9 11.3 %all-to-all-done.6 = bf16[32,32,256]{2,1,0:T(8,128)(2,1)S(1)} async-done(((bf16[32,32,256]{2,1,0:T(8,128)(2,1)}), bf16[32,32,256]{2,1,0:T(8,128)(2,1)S(1)}, u32[]{:S(2)}, u32[]{:S(2)}) %all-to-all-start.6) | async-done | bytes 524320 | tf_op jit(solution)/shard_map/all_to_all | solution.py:286
  214.2 0.8 copy.5
  (7 shorter events, 0.4 us)
Async XLA Ops:
  25.6 13.4 %collective-permute-start = (f32[128,512]{1,0:T(8,128)S(1)}, f32[128,512]{1,0:T(8,128)S(1)}, u32[]{:S(2)}, u32[]{:S(2)}) collective-permute-start(f32[128,512]{1,0:T(8,128)S(1)} %add_bitcast_fusion), channel_id=1, source_target_pairs={{0,24},{24,0},{16,40},{40,16},{32,56},{56,32},{48,8},{8,48},{64,88... | collective-permute-start | bytes 786440 | tf_op jit(solution)/shard_map/ppermute | solution.py:258
  39.1 8.2 %collective-permute-start.1 = (f32[128,512]{1,0:T(8,128)S(1)}, f32[128,512]{1,0:T(8,128)S(1)}, u32[]{:S(2)}, u32[]{:S(2)}) collective-permute-start(f32[128,512]{1,0:T(8,128)S(1)} %fusion.4), channel_id=1, source_target_pairs={{8,16},{16,8},{24,32},{32,24},{40,48},{48,40},{56,0},{0,56},{72,80... | collective-permute-start | bytes 786440 | tf_op jit(solution)/shard_map/ppermute | solution.py:258
  100.9 9.4 %collective-permute-start.2 = (bf16[128,512]{1,0:T(8,128)(2,1)S(1)}, bf16[128,512]{1,0:T(8,128)(2,1)S(1)}, u32[]{:S(2)}, u32[]{:S(2)}) collective-permute-start(bf16[128,512]{1,0:T(8,128)(2,1)S(1)} %fusion.1), channel_id=1, source_target_pairs={{0,24},{24,0},{16,40},{40,16},{32,56},{56,32},{48,8},{8,48},{64,88... | collective-permute-start | bytes 393224 | tf_op jit(solution)/shard_map/ppermute | solution.py:258
  110.5 6.5 %collective-permute-start.3 = (bf16[128,512]{1,0:T(8,128)(2,1)S(1)}, bf16[128,512]{1,0:T(8,128)(2,1)S(1)}, u32[]{:S(2)}, u32[]{:S(2)}) collective-permute-start(bf16[128,512]{1,0:T(8,128)(2,1)S(1)} %add_convert_fusion.4), channel_id=1, source_target_pairs={{8,16},{16,8},{24,32},{32,24},{40,48},{48,40},{56,0},{0,56},{72,80... | collective-permute-start | bytes 393224 | tf_op jit(solution)/shard_map/ppermute | solution.py:258
  156.1 9.2 %collective-permute-start.4 = (bf16[128,512]{1,0:T(8,128)(2,1)S(1)}, bf16[128,512]{1,0:T(8,128)(2,1)S(1)}, u32[]{:S(2)}, u32[]{:S(2)}) collective-permute-start(bf16[128,512]{1,0:T(8,128)(2,1)S(1)} %fusion.2), channel_id=1, source_target_pairs={{0,24},{24,0},{16,40},{40,16},{32,56},{56,32},{48,8},{8,48},{64,88... | collective-permute-start | bytes 393224 | tf_op jit(solution)/shard_map/ppermute | solution.py:258
  165.4 5.2 %collective-permute-start.5 = (bf16[128,512]{1,0:T(8,128)(2,1)S(1)}, bf16[128,512]{1,0:T(8,128)(2,1)S(1)}, u32[]{:S(2)}, u32[]{:S(2)}) collective-permute-start(bf16[128,512]{1,0:T(8,128)(2,1)S(1)} %add_convert_fusion.1), channel_id=1, source_target_pairs={{8,16},{16,8},{24,32},{32,24},{40,48},{48,40},{56,0},{0,56},{72,80... | collective-permute-start | bytes 393224 | tf_op jit(solution)/shard_map/ppermute | solution.py:258
  193.8 20.4 %all-to-all-start.6 = ((bf16[32,32,256]{2,1,0:T(8,128)(2,1)}), bf16[32,32,256]{2,1,0:T(8,128)(2,1)S(1)}, u32[]{:S(2)}, u32[]{:S(2)}) async-start(bf16[32,32,256]{2,1,0:T(8,128)(2,1)} %bitcast.11), calls=%async_computation.6 | async-start | bytes 1048576 | tf_op jit(solution)/shard_map/all_to_all | solution.py:286

commit v6 on v5

--- a/solution.py
+++ b/solution.py
@@ -18,7 +18,7 @@
 AXES = ("x", "z_high", "z_low", "grp")
 POS = AXES[:3]
 NEAR = [
-    [x * NZ + 2 * high + (low ^ (high % 2)) for x in range(NX) for low in range(NZ_LOW)]
+    [x * NZ + 2 * high + (low ^ (high % 2)) for low in range(NZ_LOW) for x in range(NX)]
     for high in range(NZ_HIGH)
 ]
 PAIRS = (((0, 3), (2, 5), (4, 7), (6, 1)), ((1, 2), (3, 4), (5, 6), (7, 0)))
@@ -27,8 +27,8 @@
 BF16 = jnp.bfloat16
 
 TERMS = BF16
-SUMS = F32
-PARTS = 2
+SUMS = BF16
+PARTS = 1
 
 NN = (((1,), (0,)), ((), ()))
 NT = (((1,), (1,)), ((), ()))

time: 215 us -> 195 us (0.907)
  blocking collectives: 108 us -> 94.1 us
  waiting for transfers between devices: 37.8 us -> 34.7 us
    all_to_all x3, blocking collectives: 56.3 us -> 43.6 us  [sum_and_spread(): lax.all_to_all(total, POS, 0, 0, axis_index_groups=NEAR, tiled=True)]
    ppermute x6, waiting for transfers between devices: 26.6 us -> 23.4 us  [sum_and_spread(): other = lax.ppermute(own, POS, both_ways)]
    ppermute x6, starting transfers between devices: 25.2 us -> 22.4 us  [sum_and_spread(): other = lax.ppermute(own, POS, both_ways)]
where the time goes in v6:
time: 195 us
  blocking collectives  94.1 us (48%)
  waiting for transfers between devices  34.7 us (18%)
  Pallas kernels  32.4 us (17%)
  starting transfers between devices  30.8 us (16%)
    all_to_all x3, blocking collectives, sum_and_spread(): terms = lax.all_to_all(terms, POS, 0, 0, axis_index_groups=NEAR, tiled=True)  50.6 us
    all_to_all x3, blocking collectives, sum_and_spread(): lax.all_to_all(total, POS, 0, 0, axis_index_groups=NEAR, tiled=True)  43.6 us
    pallas_call x5, Pallas kernels, call(): pl.pallas_call(body, out_shape=out_shape, in_specs=spec, out_specs=jax.tr...  32.4 us
    ppermute x6, waiting for transfers between devices, sum_and_spread(): other = lax.ppermute(own, POS, both_ways)  23.4 us
    ppermute x6, starting transfers between devices, sum_and_spread(): other = lax.ppermute(own, POS, both_ways)  22.4 us
    all_to_all x1, waiting for transfers between devices, local(): lax.all_to_all(compressed, ('x', 'z_high', 'z_low'), split_axis=0, concat...  11.3 us
    all_to_all x1, starting transfers between devices, local(): lax.all_to_all(compressed, ('x', 'z_high', 'z_low'), split_axis=0, concat...  8.38 us
  transfers between devices with their start and end apart: 7, of which 7 were waited for; matrix products, arithmetic and copies ran while one was open for 0% of the time, Pallas kernels for 1%

profile of v6, /device:TPU:56, one launch (start us, length us, event | category | flops | bytes accessed | tf_op | source)
XLA Modules:
  0.0 194.8 jit_solution(5457410587947568108)
XLA Ops:
  0.6 4.8 %shard_map.41 = bf16[4,256,512]{2,1,0:T(8,128)(2,1)S(1)} custom-call(bf16[1024,2048]{1,0:T(8,128)(2,1)} %keys_hbm.7, f32[2048,256]{1,0:T(8,128)} %basis_hbm.1), custom_call_target="tpu_custom_call" | custom-call | tf_op jit(solution)/shard_map/pallas_call | solution.py:229
  5.4 19.9 %all_to_all.42 = bf16[8,128,512]{2,1,0:T(8,128)(2,1)S(1)} all-to-all(bf16[8,128,512]{2,1,0:T(8,128)(2,1)S(1)} %bitcast.22), channel_id=1, replica_groups={{0,64,128,192,8,72,136,200},{24,88,152,216,16,80,144,208},{32,96,160,22..., dimensions={0} | all-to-all | bytes 2097152 | tf_op jit(solution)/shard_map/all_to_all | solution.py:252
  25.3 0.1 fusion
  25.4 5.9 %collective-permute-start = (bf16[128,512]{1,0:T(8,128)(2,1)S(1)}, bf16[128,512]{1,0:T(8,128)(2,1)S(1)}, u32[]{:S(2)}, u32[]{:S(2)}) collective-permute-start(bf16[128,512]{1,0:T(8,128)(2,1)S(1)} %fusion), channel_id=1, source_target_pairs={{0,24},{24,0},{16,40},{40,16},{32,56},{56,32},{48,8},{8,48},{64,88... | collective-permute-start | bytes 393224 | tf_op jit(solution)/shard_map/ppermute | solution.py:258
  31.4 4.4 %collective-permute-done = bf16[128,512]{1,0:T(8,128)(2,1)S(1)} collective-permute-done((bf16[128,512]{1,0:T(8,128)(2,1)S(1)}, bf16[128,512]{1,0:T(8,128)(2,1)S(1)}, u32[]{:S(2)}, u32[]{:S(2)}) %collective-permute-start) | collective-permute-done | bytes 131104 | tf_op jit(solution)/shard_map/ppermute | solution.py:258
  35.7 0.2 add_convert_fusion.7
  35.9 1.4 collective-permute-start.1
  37.3 3.6 %collective-permute-done.1 = bf16[128,512]{1,0:T(8,128)(2,1)S(1)} collective-permute-done((bf16[128,512]{1,0:T(8,128)(2,1)S(1)}, bf16[128,512]{1,0:T(8,128)(2,1)S(1)}, u32[]{:S(2)}, u32[]{:S(2)}) %collective-permute-start.1) | collective-permute-done | bytes 131104 | tf_op jit(solution)/shard_map/ppermute | solution.py:258
  41.1 14.9 %all_to_all.43 = bf16[8,1,128,512]{3,2,1,0:T(8,128)(2,1)S(1)} all-to-all(bf16[8,1,128,512]{3,2,1,0:T(8,128)(2,1)S(1)} %broadcast_in_dim.6), channel_id=1, replica_groups={{0,64,128,192,8,72,136,200},{24,88,152,216,16,80,144,208},{32,96,160,22..., dimensions={0} | all-to-all | bytes 2097152 | tf_op jit(solution)/shard_map/all_to_all | solution.py:262
  55.9 8.6 %shard_map.42 = bf16[4,256,512]{2,1,0:T(8,128)(2,1)S(1)} custom-call(bf16[4,2,1,128,512]{4,3,2,1,0:T(8,128)(2,1)S(1)} %bitcast.23, bf16[1024,2048]{1,0:T(8,128)(2,1)} %keys_hbm.7), custom_call_target="tpu_custom_call" | custom-call | tf_op jit(solution)/shard_map/pallas_call | solution.py:229
  64.6 16.6 %all_to_all.44 = bf16[8,128,512]{2,1,0:T(8,128)(2,1)S(1)} all-to-all(bf16[8,128,512]{2,1,0:T(8,128)(2,1)S(1)} %bitcast.24), channel_id=1, replica_groups={{0,64,128,192,8,72,136,200},{24,88,152,216,16,80,144,208},{32,96,160,22..., dimensions={0} | all-to-all | bytes 2097152 | tf_op jit(solution)/shard_map/all_to_all | solution.py:252
  81.2 0.1 fusion.1
  81.3 3.8 %collective-permute-start.2 = (bf16[128,512]{1,0:T(8,128)(2,1)S(1)}, bf16[128,512]{1,0:T(8,128)(2,1)S(1)}, u32[]{:S(2)}, u32[]{:S(2)}) collective-permute-start(bf16[128,512]{1,0:T(8,128)(2,1)S(1)} %fusion.1), channel_id=1, source_target_pairs={{0,24},{24,0},{16,40},{40,16},{32,56},{56,32},{48,8},{8,48},{64,88... | collective-permute-start | bytes 393224 | tf_op jit(solution)/shard_map/ppermute | solution.py:258
  85.1 4.5 %collective-permute-done.2 = bf16[128,512]{1,0:T(8,128)(2,1)S(1)} collective-permute-done((bf16[128,512]{1,0:T(8,128)(2,1)S(1)}, bf16[128,512]{1,0:T(8,128)(2,1)S(1)}, u32[]{:S(2)}, u32[]{:S(2)}) %collective-permute-start.2) | collective-permute-done | bytes 131104 | tf_op jit(solution)/shard_map/ppermute | solution.py:258
  89.7 0.2 add_convert_fusion.4
  89.8 2.6 %collective-permute-start.3 = (bf16[128,512]{1,0:T(8,128)(2,1)S(1)}, bf16[128,512]{1,0:T(8,128)(2,1)S(1)}, u32[]{:S(2)}, u32[]{:S(2)}) collective-permute-start(bf16[128,512]{1,0:T(8,128)(2,1)S(1)} %add_convert_fusion.4), channel_id=1, source_target_pairs={{8,16},{16,8},{24,32},{32,24},{40,48},{48,40},{56,0},{0,56},{72,80... | collective-permute-start | bytes 393224 | tf_op jit(solution)/shard_map/ppermute | solution.py:258
  92.4 2.9 %collective-permute-done.3 = bf16[128,512]{1,0:T(8,128)(2,1)S(1)} collective-permute-done((bf16[128,512]{1,0:T(8,128)(2,1)S(1)}, bf16[128,512]{1,0:T(8,128)(2,1)S(1)}, u32[]{:S(2)}, u32[]{:S(2)}) %collective-permute-start.3) | collective-permute-done | bytes 131104 | tf_op jit(solution)/shard_map/ppermute | solution.py:258
  95.5 14.4 %all_to_all.45 = bf16[8,1,128,512]{3,2,1,0:T(8,128)(2,1)S(1)} all-to-all(bf16[8,1,128,512]{3,2,1,0:T(8,128)(2,1)S(1)} %broadcast_in_dim.7), channel_id=1, replica_groups={{0,64,128,192,8,72,136,200},{24,88,152,216,16,80,144,208},{32,96,160,22..., dimensions={0} | all-to-all | bytes 2097152 | tf_op jit(solution)/shard_map/all_to_all | solution.py:262
  109.9 8.6 %shard_map.43 = bf16[4,256,512]{2,1,0:T(8,128)(2,1)S(1)} custom-call(bf16[4,2,1,128,512]{4,3,2,1,0:T(8,128)(2,1)S(1)} %bitcast.25, bf16[1024,2048]{1,0:T(8,128)(2,1)} %keys_hbm.7), custom_call_target="tpu_custom_call" | custom-call | tf_op jit(solution)/shard_map/pallas_call | solution.py:229
  118.5 14.1 %all_to_all.46 = bf16[8,128,512]{2,1,0:T(8,128)(2,1)S(1)} all-to-all(bf16[8,128,512]{2,1,0:T(8,128)(2,1)S(1)} %bitcast.26), channel_id=1, replica_groups={{0,64,128,192,8,72,136,200},{24,88,152,216,16,80,144,208},{32,96,160,22..., dimensions={0} | all-to-all | bytes 2097152 | tf_op jit(solution)/shard_map/all_to_all | solution.py:252
  132.5 0.1 fusion.2
  132.7 4.5 %collective-permute-start.4 = (bf16[128,512]{1,0:T(8,128)(2,1)S(1)}, bf16[128,512]{1,0:T(8,128)(2,1)S(1)}, u32[]{:S(2)}, u32[]{:S(2)}) collective-permute-start(bf16[128,512]{1,0:T(8,128)(2,1)S(1)} %fusion.2), channel_id=1, source_target_pairs={{0,24},{24,0},{16,40},{40,16},{32,56},{56,32},{48,8},{8,48},{64,88... | collective-permute-start | bytes 393224 | tf_op jit(solution)/shard_map/ppermute | solution.py:258
  137.1 5.0 %collective-permute-done.4 = bf16[128,512]{1,0:T(8,128)(2,1)S(1)} collective-permute-done((bf16[128,512]{1,0:T(8,128)(2,1)S(1)}, bf16[128,512]{1,0:T(8,128)(2,1)S(1)}, u32[]{:S(2)}, u32[]{:S(2)}) %collective-permute-start.4) | collective-permute-done | bytes 131104 | tf_op jit(solution)/shard_map/ppermute | solution.py:258
  142.1 0.2 add_convert_fusion.1
  142.3 4.2 %collective-permute-start.5 = (bf16[128,512]{1,0:T(8,128)(2,1)S(1)}, bf16[128,512]{1,0:T(8,128)(2,1)S(1)}, u32[]{:S(2)}, u32[]{:S(2)}) collective-permute-start(bf16[128,512]{1,0:T(8,128)(2,1)S(1)} %add_convert_fusion.1), channel_id=1, source_target_pairs={{8,16},{16,8},{24,32},{32,24},{40,48},{48,40},{56,0},{0,56},{72,80... | collective-permute-start | bytes 393224 | tf_op jit(solution)/shard_map/ppermute | solution.py:258
  146.5 2.9 %collective-permute-done.5 = bf16[128,512]{1,0:T(8,128)(2,1)S(1)} collective-permute-done((bf16[128,512]{1,0:T(8,128)(2,1)S(1)}, bf16[128,512]{1,0:T(8,128)(2,1)S(1)}, u32[]{:S(2)}, u32[]{:S(2)}) %collective-permute-start.5) | collective-permute-done | bytes 131104 | tf_op jit(solution)/shard_map/ppermute | solution.py:258
  149.6 14.3 %all_to_all.47 = bf16[8,1,128,512]{3,2,1,0:T(8,128)(2,1)S(1)} all-to-all(bf16[8,1,128,512]{3,2,1,0:T(8,128)(2,1)S(1)} %broadcast_in_dim.8), channel_id=1, replica_groups={{0,64,128,192,8,72,136,200},{24,88,152,216,16,80,144,208},{32,96,160,22..., dimensions={0} | all-to-all | bytes 2097152 | tf_op jit(solution)/shard_map/all_to_all | solution.py:262
  164.0 8.3 %shard_map.44 = (f32[256,256]{1,0:T(8,128)S(1)}, bf16[1024,256]{1,0:T(8,128)(2,1)}) custom-call(bf16[4,256,512]{2,1,0:T(8,128)(2,1)S(1)} %bitcast.20, bf16[1024,2048]{1,0:T(8,128)(2,1)} %keys_hbm.7), custom_call_target="tpu_custom_call" | custom-call | tf_op jit(solution)/shard_map/pallas_call | solution.py:229
  172.2 8.4 %all-to-all-start.6 = ((bf16[32,32,256]{2,1,0:T(8,128)(2,1)}), bf16[32,32,256]{2,1,0:T(8,128)(2,1)S(1)}, u32[]{:S(2)}, u32[]{:S(2)}) async-start(bf16[32,32,256]{2,1,0:T(8,128)(2,1)} %bitcast.9), calls=%async_computation.6 | async-start | bytes 1048576 | tf_op jit(solution)/shard_map/all_to_all | solution.py:286
  180.6 2.2 %shard_map.45 = f32[2048,256]{1,0:T(8,128)} custom-call(bf16[4,256,512]{2,1,0:T(8,128)(2,1)S(1)} %bitcast.21, f32[256,256]{1,0:T(8,128)S(1)} %get-tuple-element.4.inv), custom_call_target="tpu_custom_call" | custom-call | flops 536870912 | bytes 4194304 | tf_op jit(solution)/shard_map/pallas_call | solution.py:229
  182.8 11.3 %all-to-all-done.6 = bf16[32,32,256]{2,1,0:T(8,128)(2,1)S(1)} async-done(((bf16[32,32,256]{2,1,0:T(8,128)(2,1)}), bf16[32,32,256]{2,1,0:T(8,128)(2,1)S(1)}, u32[]{:S(2)}, u32[]{:S(2)}) %all-to-all-start.6) | async-done | bytes 524320 | tf_op jit(solution)/shard_map/all_to_all | solution.py:286
  194.0 0.8 copy.5
  (6 shorter events, 0.3 us)
Async XLA Ops:
  25.4 10.3 %collective-permute-start = (bf16[128,512]{1,0:T(8,128)(2,1)S(1)}, bf16[128,512]{1,0:T(8,128)(2,1)S(1)}, u32[]{:S(2)}, u32[]{:S(2)}) collective-permute-start(bf16[128,512]{1,0:T(8,128)(2,1)S(1)} %fusion), channel_id=1, source_target_pairs={{0,24},{24,0},{16,40},{40,16},{32,56},{56,32},{48,8},{8,48},{64,88... | collective-permute-start | bytes 393224 | tf_op jit(solution)/shard_map/ppermute | solution.py:258
  35.9 5.1 %collective-permute-start.1 = (bf16[128,512]{1,0:T(8,128)(2,1)S(1)}, bf16[128,512]{1,0:T(8,128)(2,1)S(1)}, u32[]{:S(2)}, u32[]{:S(2)}) collective-permute-start(bf16[128,512]{1,0:T(8,128)(2,1)S(1)} %add_convert_fusion.7), channel_id=1, source_target_pairs={{8,16},{16,8},{24,32},{32,24},{40,48},{48,40},{56,0},{0,56},{72,80... | collective-permute-start | bytes 393224 | tf_op jit(solution)/shard_map/ppermute | solution.py:258
  81.3 8.3 %collective-permute-start.2 = (bf16[128,512]{1,0:T(8,128)(2,1)S(1)}, bf16[128,512]{1,0:T(8,128)(2,1)S(1)}, u32[]{:S(2)}, u32[]{:S(2)}) collective-permute-start(bf16[128,512]{1,0:T(8,128)(2,1)S(1)} %fusion.1), channel_id=1, source_target_pairs={{0,24},{24,0},{16,40},{40,16},{32,56},{56,32},{48,8},{8,48},{64,88... | collective-permute-start | bytes 393224 | tf_op jit(solution)/shard_map/ppermute | solution.py:258
  89.8 5.5 %collective-permute-start.3 = (bf16[128,512]{1,0:T(8,128)(2,1)S(1)}, bf16[128,512]{1,0:T(8,128)(2,1)S(1)}, u32[]{:S(2)}, u32[]{:S(2)}) collective-permute-start(bf16[128,512]{1,0:T(8,128)(2,1)S(1)} %add_convert_fusion.4), channel_id=1, source_target_pairs={{8,16},{16,8},{24,32},{32,24},{40,48},{48,40},{56,0},{0,56},{72,80... | collective-permute-start | bytes 393224 | tf_op jit(solution)/shard_map/ppermute | solution.py:258
  132.7 9.5 %collective-permute-start.4 = (bf16[128,512]{1,0:T(8,128)(2,1)S(1)}, bf16[128,512]{1,0:T(8,128)(2,1)S(1)}, u32[]{:S(2)}, u32[]{:S(2)}) collective-permute-start(bf16[128,512]{1,0:T(8,128)(2,1)S(1)} %fusion.2), channel_id=1, source_target_pairs={{0,24},{24,0},{16,40},{40,16},{32,56},{56,32},{48,8},{8,48},{64,88... | collective-permute-start | bytes 393224 | tf_op jit(solution)/shard_map/ppermute | solution.py:258
  142.3 7.2 %collective-permute-start.5 = (bf16[128,512]{1,0:T(8,128)(2,1)S(1)}, bf16[128,512]{1,0:T(8,128)(2,1)S(1)}, u32[]{:S(2)}, u32[]{:S(2)}) collective-permute-start(bf16[128,512]{1,0:T(8,128)(2,1)S(1)} %add_convert_fusion.1), channel_id=1, source_target_pairs={{8,16},{16,8},{24,32},{32,24},{40,48},{48,40},{56,0},{0,56},{72,80... | collective-permute-start | bytes 393224 | tf_op jit(solution)/shard_map/ppermute | solution.py:258
  172.2 21.8 %all-to-all-start.6 = ((bf16[32,32,256]{2,1,0:T(8,128)(2,1)}), bf16[32,32,256]{2,1,0:T(8,128)(2,1)S(1)}, u32[]{:S(2)}, u32[]{:S(2)}) async-start(bf16[32,32,256]{2,1,0:T(8,128)(2,1)} %bitcast.9), calls=%async_computation.6 | async-start | bytes 1048576 | tf_op jit(solution)/shard_map/all_to_all | solution.py:286

commit v7 on v5

--- a/solution.py
+++ b/solution.py
@@ -18,7 +18,7 @@
 AXES = ("x", "z_high", "z_low", "grp")
 POS = AXES[:3]
 NEAR = [
-    [x * NZ + 2 * high + (low ^ (high % 2)) for x in range(NX) for low in range(NZ_LOW)]
+    [x * NZ + 2 * high + (low ^ (high % 2)) for low in range(NZ_LOW) for x in range(NX)]
     for high in range(NZ_HIGH)
 ]
 PAIRS = (((0, 3), (2, 5), (4, 7), (6, 1)), ((1, 2), (3, 4), (5, 6), (7, 0)))
@@ -26,7 +26,6 @@
 F32 = jnp.float32
 BF16 = jnp.bfloat16
 
-TERMS = BF16
 SUMS = F32
 PARTS = 2
 
@@ -274,9 +273,9 @@
     blocks = shape((NX, rank, width), BF16)
 
     scratch = [keys, pltpu.VMEM((features, rank), F32), sem((NX,)), sem((NX,))]
-    term = call(first_kernel, shape((NX, rank, width), TERMS), (key_cache, init_basis), (True, True), scratch)
+    term = call(first_kernel, blocks, (key_cache, init_basis), (True, True), scratch)
     for sweep in range(ITERS - 1):
-        summed = sum_and_spread(term, *((SUMS, PARTS) if sweep == 0 else (BF16, 1)))
+        summed = sum_and_spread(term, SUMS, PARTS)
         scratch = [square, square, pltpu.VMEM((rank, positions), F32), keys, sem]
         term = call(middle_kernel, blocks, (summed, key_cache), (False, True), scratch)
     summed = sum_and_spread(term, BF16, 1).reshape(NX, rank, width)

time: 215 us -> 232 us (1.079)
  waiting for transfers between devices: 37.8 us -> 46.9 us
  blocking collectives: 108 us -> 117 us
  starting transfers between devices: 32.2 us -> 27.5 us
    all_to_all x3, blocking collectives: 56.3 us -> 66.2 us  [sum_and_spread(): lax.all_to_all(total, POS, 0, 0, axis_index_groups=NEAR, tiled=True)]
    ppermute x6, waiting for transfers between devices: 26.6 us -> 35.6 us  [sum_and_spread(): other = lax.ppermute(own, POS, both_ways)]
    ppermute x6, starting transfers between devices: 25.2 us -> 20.1 us  [sum_and_spread(): other = lax.ppermute(own, POS, both_ways)]
where the time goes in v7:
time: 232 us; the launch traced here: 231 us
  blocking collectives  117 us (50%)
  waiting for transfers between devices  46.9 us (20%)
  Pallas kernels  36.6 us (16%)
  starting transfers between devices  27.5 us (12%)
    all_to_all x3, blocking collectives, sum_and_spread(): lax.all_to_all(total, POS, 0, 0, axis_index_groups=NEAR, tiled=True)  66.2 us
    all_to_all x3, blocking collectives, sum_and_spread(): terms = lax.all_to_all(terms, POS, 0, 0, axis_index_groups=NEAR, tiled=True)  50.9 us
    pallas_call x5, Pallas kernels, call(): pl.pallas_call(body, out_shape=out_shape, in_specs=spec, out_specs=jax.tr...  36.6 us
    ppermute x6, waiting for transfers between devices, sum_and_spread(): other = lax.ppermute(own, POS, both_ways)  35.6 us
    ppermute x6, starting transfers between devices, sum_and_spread(): other = lax.ppermute(own, POS, both_ways)  20.1 us
    all_to_all x1, waiting for transfers between devices, local(): lax.all_to_all(compressed, ('x', 'z_high', 'z_low'), split_axis=0, concat...  11.3 us
    all_to_all x1, starting transfers between devices, local(): lax.all_to_all(compressed, ('x', 'z_high', 'z_low'), split_axis=0, concat...  7.36 us
  transfers between devices with their start and end apart: 7, of which 7 were waited for; matrix products, arithmetic and copies ran while one was open for 0% of the time, Pallas kernels for 1%

profile of v7, /device:TPU:56, one launch (start us, length us, event | category | flops | bytes accessed | tf_op | source)
XLA Modules:
  0.0 231.1 jit_solution(7954100290324804954)
XLA Ops:
  0.6 4.8 %shard_map.41 = bf16[4,256,512]{2,1,0:T(8,128)(2,1)S(1)} custom-call(bf16[1024,2048]{1,0:T(8,128)(2,1)} %keys_hbm.7, f32[2048,256]{1,0:T(8,128)} %basis_hbm.1), custom_call_target="tpu_custom_call" | custom-call | tf_op jit(solution)/shard_map/pallas_call | solution.py:228
  5.4 19.9 %all_to_all.42 = bf16[8,128,512]{2,1,0:T(8,128)(2,1)S(1)} all-to-all(bf16[8,128,512]{2,1,0:T(8,128)(2,1)S(1)} %bitcast.32), channel_id=1, replica_groups={{0,64,128,192,8,72,136,200},{24,88,152,216,16,80,144,208},{32,96,160,22..., dimensions={0} | all-to-all | bytes 2097152 | tf_op jit(solution)/shard_map/all_to_all | solution.py:251
  25.4 5.9 %collective-permute-start = (f32[128,512]{1,0:T(8,128)S(1)}, f32[128,512]{1,0:T(8,128)S(1)}, u32[]{:S(2)}, u32[]{:S(2)}) collective-permute-start(f32[128,512]{1,0:T(8,128)S(1)} %add_bitcast_fusion.1), channel_id=1, source_target_pairs={{0,24},{24,0},{16,40},{40,16},{32,56},{56,32},{48,8},{8,48},{64,88... | collective-permute-start | bytes 786440 | tf_op jit(solution)/shard_map/ppermute | solution.py:257
  31.4 10.1 %collective-permute-done = f32[128,512]{1,0:T(8,128)S(1)} collective-permute-done((f32[128,512]{1,0:T(8,128)S(1)}, f32[128,512]{1,0:T(8,128)S(1)}, u32[]{:S(2)}, u32[]{:S(2)}) %collective-permute-start) | collective-permute-done | bytes 262176 | tf_op jit(solution)/shard_map/ppermute | solution.py:257
  41.4 0.1 fusion.6
  41.6 1.3 collective-permute-start.1
  42.8 5.2 %collective-permute-done.1 = f32[128,512]{1,0:T(8,128)S(1)} collective-permute-done((f32[128,512]{1,0:T(8,128)S(1)}, f32[128,512]{1,0:T(8,128)S(1)}, u32[]{:S(2)}, u32[]{:S(2)}) %collective-permute-start.1) | collective-permute-done | bytes 262176 | tf_op jit(solution)/shard_map/ppermute | solution.py:257
  48.1 0.2 broadcast_in_dim.6
  48.3 26.9 %all_to_all.43 = bf16[8,2,128,512]{3,2,1,0:T(8,128)(2,1)} all-to-all(bf16[8,2,128,512]{3,2,1,0:T(8,128)(2,1)S(1)} %broadcast_in_dim.6), channel_id=1, replica_groups={{0,64,128,192,8,72,136,200},{24,88,152,216,16,80,144,208},{32,96,160,22..., dimensions={0} | all-to-all | bytes 4194304 | tf_op jit(solution)/shard_map/all_to_all | solution.py:261
  75.3 10.7 %shard_map.42 = bf16[4,256,512]{2,1,0:T(8,128)(2,1)S(1)} custom-call(bf16[4,2,2,128,512]{4,3,2,1,0:T(8,128)(2,1)} %bitcast.33, bf16[1024,2048]{1,0:T(8,128)(2,1)} %keys_hbm.7), custom_call_target="tpu_custom_call" | custom-call | tf_op jit(solution)/shard_map/pallas_call | solution.py:228
  86.0 14.2 %all_to_all.44 = bf16[8,128,512]{2,1,0:T(8,128)(2,1)S(1)} all-to-all(bf16[8,128,512]{2,1,0:T(8,128)(2,1)S(1)} %bitcast.30), channel_id=1, replica_groups={{0,64,128,192,8,72,136,200},{24,88,152,216,16,80,144,208},{32,96,160,22..., dimensions={0} | all-to-all | bytes 2097152 | tf_op jit(solution)/shard_map/all_to_all | solution.py:251
  100.3 6.1 %collective-permute-start.2 = (f32[128,512]{1,0:T(8,128)S(1)}, f32[128,512]{1,0:T(8,128)S(1)}, u32[]{:S(2)}, u32[]{:S(2)}) collective-permute-start(f32[128,512]{1,0:T(8,128)S(1)} %add_bitcast_fusion), channel_id=1, source_target_pairs={{0,24},{24,0},{16,40},{40,16},{32,56},{56,32},{48,8},{8,48},{64,88... | collective-permute-start | bytes 786440 | tf_op jit(solution)/shard_map/ppermute | solution.py:257
  106.5 4.5 %collective-permute-done.2 = f32[128,512]{1,0:T(8,128)S(1)} collective-permute-done((f32[128,512]{1,0:T(8,128)S(1)}, f32[128,512]{1,0:T(8,128)S(1)}, u32[]{:S(2)}, u32[]{:S(2)}) %collective-permute-start.2) | collective-permute-done | bytes 262176 | tf_op jit(solution)/shard_map/ppermute | solution.py:257
  110.9 0.1 fusion.5
  111.1 3.8 %collective-permute-start.3 = (f32[128,512]{1,0:T(8,128)S(1)}, f32[128,512]{1,0:T(8,128)S(1)}, u32[]{:S(2)}, u32[]{:S(2)}) collective-permute-start(f32[128,512]{1,0:T(8,128)S(1)} %fusion.5), channel_id=1, source_target_pairs={{8,16},{16,8},{24,32},{32,24},{40,48},{48,40},{56,0},{0,56},{72,80... | collective-permute-start | bytes 786440 | tf_op jit(solution)/shard_map/ppermute | solution.py:257
  114.9 4.4 %collective-permute-done.3 = f32[128,512]{1,0:T(8,128)S(1)} collective-permute-done((f32[128,512]{1,0:T(8,128)S(1)}, f32[128,512]{1,0:T(8,128)S(1)}, u32[]{:S(2)}, u32[]{:S(2)}) %collective-permute-start.3) | collective-permute-done | bytes 262176 | tf_op jit(solution)/shard_map/ppermute | solution.py:257
  119.3 0.2 broadcast_in_dim.7
  119.5 26.1 %all_to_all.45 = bf16[8,2,128,512]{3,2,1,0:T(8,128)(2,1)} all-to-all(bf16[8,2,128,512]{3,2,1,0:T(8,128)(2,1)S(1)} %broadcast_in_dim.7), channel_id=1, replica_groups={{0,64,128,192,8,72,136,200},{24,88,152,216,16,80,144,208},{32,96,160,22..., dimensions={0} | all-to-all | bytes 4194304 | tf_op jit(solution)/shard_map/all_to_all | solution.py:261
  145.7 10.7 %shard_map.43 = bf16[4,256,512]{2,1,0:T(8,128)(2,1)S(1)} custom-call(bf16[4,2,2,128,512]{4,3,2,1,0:T(8,128)(2,1)} %bitcast.34, bf16[1024,2048]{1,0:T(8,128)(2,1)} %keys_hbm.7), custom_call_target="tpu_custom_call" | custom-call | tf_op jit(solution)/shard_map/pallas_call | solution.py:228
  156.4 16.8 %all_to_all.46 = bf16[8,128,512]{2,1,0:T(8,128)(2,1)S(1)} all-to-all(bf16[8,128,512]{2,1,0:T(8,128)(2,1)S(1)} %bitcast.31), channel_id=1, replica_groups={{0,64,128,192,8,72,136,200},{24,88,152,216,16,80,144,208},{32,96,160,22..., dimensions={0} | all-to-all | bytes 2097152 | tf_op jit(solution)/shard_map/all_to_all | solution.py:251
  173.2 0.1 fusion.2
  173.3 1.1 collective-permute-start.4
  174.4 8.4 %collective-permute-done.4 = bf16[128,512]{1,0:T(8,128)(2,1)S(1)} collective-permute-done((bf16[128,512]{1,0:T(8,128)(2,1)S(1)}, bf16[128,512]{1,0:T(8,128)(2,1)S(1)}, u32[]{:S(2)}, u32[]{:S(2)}) %collective-permute-start.4) | collective-permute-done | bytes 131104 | tf_op jit(solution)/shard_map/ppermute | solution.py:257
  182.8 0.2 add_convert_fusion.1
  183.0 1.9 collective-permute-start.5
  184.8 3.2 %collective-permute-done.5 = bf16[128,512]{1,0:T(8,128)(2,1)S(1)} collective-permute-done((bf16[128,512]{1,0:T(8,128)(2,1)S(1)}, bf16[128,512]{1,0:T(8,128)(2,1)S(1)}, u32[]{:S(2)}, u32[]{:S(2)}) %collective-permute-start.5) | collective-permute-done | bytes 131104 | tf_op jit(solution)/shard_map/ppermute | solution.py:257
  188.1 13.1 %all_to_all.47 = bf16[8,1,128,512]{3,2,1,0:T(8,128)(2,1)S(1)} all-to-all(bf16[8,1,128,512]{3,2,1,0:T(8,128)(2,1)S(1)} %broadcast_in_dim.8), channel_id=1, replica_groups={{0,64,128,192,8,72,136,200},{24,88,152,216,16,80,144,208},{32,96,160,22..., dimensions={0} | all-to-all | bytes 2097152 | tf_op jit(solution)/shard_map/all_to_all | solution.py:261
  201.3 8.2 %shard_map.44 = (f32[256,256]{1,0:T(8,128)S(1)}, bf16[1024,256]{1,0:T(8,128)(2,1)}) custom-call(bf16[4,256,512]{2,1,0:T(8,128)(2,1)S(1)} %bitcast.28, bf16[1024,2048]{1,0:T(8,128)(2,1)} %keys_hbm.7), custom_call_target="tpu_custom_call" | custom-call | tf_op jit(solution)/shard_map/pallas_call | solution.py:228
  209.5 7.4 %all-to-all-start.6 = ((bf16[32,32,256]{2,1,0:T(8,128)(2,1)}), bf16[32,32,256]{2,1,0:T(8,128)(2,1)S(1)}, u32[]{:S(2)}, u32[]{:S(2)}) async-start(bf16[32,32,256]{2,1,0:T(8,128)(2,1)} %bitcast.13), calls=%async_computation.6 | async-start | bytes 1048576 | tf_op jit(solution)/shard_map/all_to_all | solution.py:285
  216.9 2.2 shard_map.45
  219.1 11.3 %all-to-all-done.6 = bf16[32,32,256]{2,1,0:T(8,128)(2,1)S(1)} async-done(((bf16[32,32,256]{2,1,0:T(8,128)(2,1)}), bf16[32,32,256]{2,1,0:T(8,128)(2,1)S(1)}, u32[]{:S(2)}, u32[]{:S(2)}) %all-to-all-start.6) | async-done | bytes 524320 | tf_op jit(solution)/shard_map/all_to_all | solution.py:285
  230.3 0.8 copy.5
  (8 shorter events, 0.5 us)
Async XLA Ops:
  25.4 16.0 %collective-permute-start = (f32[128,512]{1,0:T(8,128)S(1)}, f32[128,512]{1,0:T(8,128)S(1)}, u32[]{:S(2)}, u32[]{:S(2)}) collective-permute-start(f32[128,512]{1,0:T(8,128)S(1)} %add_bitcast_fusion.1), channel_id=1, source_target_pairs={{0,24},{24,0},{16,40},{40,16},{32,56},{56,32},{48,8},{8,48},{64,88... | collective-permute-start | bytes 786440 | tf_op jit(solution)/shard_map/ppermute | solution.py:257
  41.6 6.5 %collective-permute-start.1 = (f32[128,512]{1,0:T(8,128)S(1)}, f32[128,512]{1,0:T(8,128)S(1)}, u32[]{:S(2)}, u32[]{:S(2)}) collective-permute-start(f32[128,512]{1,0:T(8,128)S(1)} %fusion.6), channel_id=1, source_target_pairs={{8,16},{16,8},{24,32},{32,24},{40,48},{48,40},{56,0},{0,56},{72,80... | collective-permute-start | bytes 786440 | tf_op jit(solution)/shard_map/ppermute | solution.py:257
  100.3 10.6 %collective-permute-start.2 = (f32[128,512]{1,0:T(8,128)S(1)}, f32[128,512]{1,0:T(8,128)S(1)}, u32[]{:S(2)}, u32[]{:S(2)}) collective-permute-start(f32[128,512]{1,0:T(8,128)S(1)} %add_bitcast_fusion), channel_id=1, source_target_pairs={{0,24},{24,0},{16,40},{40,16},{32,56},{56,32},{48,8},{8,48},{64,88... | collective-permute-start | bytes 786440 | tf_op jit(solution)/shard_map/ppermute | solution.py:257
  111.1 8.2 %collective-permute-start.3 = (f32[128,512]{1,0:T(8,128)S(1)}, f32[128,512]{1,0:T(8,128)S(1)}, u32[]{:S(2)}, u32[]{:S(2)}) collective-permute-start(f32[128,512]{1,0:T(8,128)S(1)} %fusion.5), channel_id=1, source_target_pairs={{8,16},{16,8},{24,32},{32,24},{40,48},{48,40},{56,0},{0,56},{72,80... | collective-permute-start | bytes 786440 | tf_op jit(solution)/shard_map/ppermute | solution.py:257
  173.3 9.5 %collective-permute-start.4 = (bf16[128,512]{1,0:T(8,128)(2,1)S(1)}, bf16[128,512]{1,0:T(8,128)(2,1)S(1)}, u32[]{:S(2)}, u32[]{:S(2)}) collective-permute-start(bf16[128,512]{1,0:T(8,128)(2,1)S(1)} %fusion.2), channel_id=1, source_target_pairs={{0,24},{24,0},{16,40},{40,16},{32,56},{56,32},{48,8},{8,48},{64,88... | collective-permute-start | bytes 393224 | tf_op jit(solution)/shard_map/ppermute | solution.py:257
  183.0 5.1 %collective-permute-start.5 = (bf16[128,512]{1,0:T(8,128)(2,1)S(1)}, bf16[128,512]{1,0:T(8,128)(2,1)S(1)}, u32[]{:S(2)}, u32[]{:S(2)}) collective-permute-start(bf16[128,512]{1,0:T(8,128)(2,1)S(1)} %add_convert_fusion.1), channel_id=1, source_target_pairs={{8,16},{16,8},{24,32},{32,24},{40,48},{48,40},{56,0},{0,56},{72,80... | collective-permute-start | bytes 393224 | tf_op jit(solution)/shard_map/ppermute | solution.py:257
  209.5 20.8 %all-to-all-start.6 = ((bf16[32,32,256]{2,1,0:T(8,128)(2,1)}), bf16[32,32,256]{2,1,0:T(8,128)(2,1)S(1)}, u32[]{:S(2)}, u32[]{:S(2)}) async-start(bf16[32,32,256]{2,1,0:T(8,128)(2,1)} %bitcast.13), calls=%async_computation.6 | async-start | bytes 1048576 | tf_op jit(solution)/shard_map/all_to_all | solution.py:285

commit v8 on v7

--- a/solution.py
+++ b/solution.py
@@ -270,14 +270,14 @@
     square = pltpu.VMEM((rank, rank), F32)
     keys = pltpu.VMEM((positions, features), BF16)
     sem = pltpu.SemaphoreType.DMA
-    blocks = shape((NX, rank, width), BF16)
+    blocks = [shape((NX, rank, width), SUMS)] * (ITERS - 1) + [shape((NX, rank, width), BF16)]
 
     scratch = [keys, pltpu.VMEM((features, rank), F32), sem((NX,)), sem((NX,))]
-    term = call(first_kernel, blocks, (key_cache, init_basis), (True, True), scratch)
+    term = call(first_kernel, blocks[0], (key_cache, init_basis), (True, True), scratch)
     for sweep in range(ITERS - 1):
         summed = sum_and_spread(term, SUMS, PARTS)
         scratch = [square, square, pltpu.VMEM((rank, positions), F32), keys, sem]
-        term = call(middle_kernel, blocks, (summed, key_cache), (False, True), scratch)
+        term = call(middle_kernel, blocks[sweep + 1], (summed, key_cache), (False, True), scratch)
     summed = sum_and_spread(term, BF16, 1).reshape(NX, rank, width)
     outs = (shape((rank, rank), F32), shape((positions, rank), BF16))
     scratch = [square, pltpu.VMEM((positions, rank), F32), keys, sem]

time: 232 us -> 253 us (1.091)
  blocking collectives: 117 us -> 137 us
  starting transfers between devices: 27.5 us -> 30.9 us
    all_to_all x3, blocking collectives: 50.9 us -> 72.1 us  [sum_and_spread(): terms = lax.all_to_all(terms, POS, 0, 0, axis_index_groups=NEAR, tiled=True)]
    ppermute x6, starting transfers between devices: 20.1 us -> 23.9 us  [sum_and_spread(): other = lax.ppermute(own, POS, both_ways)]
where the time goes in v8:
time: 253 us
  blocking collectives  137 us (54%)
  waiting for transfers between devices  44.4 us (18%)
  Pallas kernels  36.6 us (14%)
  starting transfers between devices  30.9 us (12%)
    all_to_all x3, blocking collectives, sum_and_spread(): terms = lax.all_to_all(terms, POS, 0, 0, axis_index_groups=NEAR, tiled=True)  72.1 us
    all_to_all x3, blocking collectives, sum_and_spread(): lax.all_to_all(total, POS, 0, 0, axis_index_groups=NEAR, tiled=True)  65.3 us
    pallas_call x5, Pallas kernels, call(): pl.pallas_call(body, out_shape=out_shape, in_specs=spec, out_specs=jax.tr...  36.6 us
    ppermute x6, waiting for transfers between devices, sum_and_spread(): other = lax.ppermute(own, POS, both_ways)  33.2 us
    ppermute x6, starting transfers between devices, sum_and_spread(): other = lax.ppermute(own, POS, both_ways)  23.9 us
    all_to_all x1, waiting for transfers between devices, local(): lax.all_to_all(compressed, ('x', 'z_high', 'z_low'), split_axis=0, concat...  11.3 us
    all_to_all x1, starting transfers between devices, local(): lax.all_to_all(compressed, ('x', 'z_high', 'z_low'), split_axis=0, concat...  7.03 us
  transfers between devices with their start and end apart: 7, of which 7 were waited for; matrix products, arithmetic and copies ran while one was open for 0% of the time, Pallas kernels for 1%

profile of v8, /device:TPU:56, one launch (start us, length us, event | category | flops | bytes accessed | tf_op | source)
XLA Modules:
  0.0 252.8 jit_solution(17146237787991630361)
XLA Ops:
  0.6 4.8 %shard_map.41 = f32[4,256,512]{2,1,0:T(8,128)S(1)} custom-call(bf16[1024,2048]{1,0:T(8,128)(2,1)} %keys_hbm.7, f32[2048,256]{1,0:T(8,128)} %basis_hbm.1), custom_call_target="tpu_custom_call" | custom-call | tf_op jit(solution)/shard_map/pallas_call | solution.py:228
  5.4 31.3 %all_to_all.42 = f32[8,128,512]{2,1,0:T(8,128)S(1)} all-to-all(f32[8,128,512]{2,1,0:T(8,128)S(1)} %bitcast.31), channel_id=1, replica_groups={{0,64,128,192,8,72,136,200},{24,88,152,216,16,80,144,208},{32,96,160,22..., dimensions={0} | all-to-all | bytes 4194304 | tf_op jit(solution)/shard_map/all_to_all | solution.py:251
  36.7 0.2 fusion.6
  36.9 5.9 %collective-permute-start = (f32[128,512]{1,0:T(8,128)S(1)}, f32[128,512]{1,0:T(8,128)S(1)}, u32[]{:S(2)}, u32[]{:S(2)}) collective-permute-start(f32[128,512]{1,0:T(8,128)S(1)} %fusion.6), channel_id=1, source_target_pairs={{0,24},{24,0},{16,40},{40,16},{32,56},{56,32},{48,8},{8,48},{64,88... | collective-permute-start | bytes 786440 | tf_op jit(solution)/shard_map/ppermute | solution.py:257
  42.9 6.7 %collective-permute-done = f32[128,512]{1,0:T(8,128)S(1)} collective-permute-done((f32[128,512]{1,0:T(8,128)S(1)}, f32[128,512]{1,0:T(8,128)S(1)}, u32[]{:S(2)}, u32[]{:S(2)}) %collective-permute-start) | collective-permute-done | bytes 262176 | tf_op jit(solution)/shard_map/ppermute | solution.py:257
  49.6 0.3 fusion.14
  49.8 1.3 collective-permute-start.1
  51.1 5.1 %collective-permute-done.1 = f32[128,512]{1,0:T(8,128)S(1)} collective-permute-done((f32[128,512]{1,0:T(8,128)S(1)}, f32[128,512]{1,0:T(8,128)S(1)}, u32[]{:S(2)}, u32[]{:S(2)}) %collective-permute-start.1) | collective-permute-done | bytes 262176 | tf_op jit(solution)/shard_map/ppermute | solution.py:257
  56.4 0.2 broadcast_in_dim.6
  56.6 29.2 %all_to_all.43 = bf16[8,2,128,512]{3,2,1,0:T(8,128)(2,1)} all-to-all(bf16[8,2,128,512]{3,2,1,0:T(8,128)(2,1)S(1)} %broadcast_in_dim.6), channel_id=1, replica_groups={{0,64,128,192,8,72,136,200},{24,88,152,216,16,80,144,208},{32,96,160,22..., dimensions={0} | all-to-all | bytes 4194304 | tf_op jit(solution)/shard_map/all_to_all | solution.py:261
  85.8 10.7 %shard_map.42 = f32[4,256,512]{2,1,0:T(8,128)S(1)} custom-call(bf16[4,2,2,128,512]{4,3,2,1,0:T(8,128)(2,1)} %bitcast.34, bf16[1024,2048]{1,0:T(8,128)(2,1)} %keys_hbm.7), custom_call_target="tpu_custom_call" | custom-call | tf_op jit(solution)/shard_map/pallas_call | solution.py:228
  96.6 24.0 %all_to_all.44 = f32[8,128,512]{2,1,0:T(8,128)S(1)} all-to-all(f32[8,128,512]{2,1,0:T(8,128)S(1)} %bitcast.30), channel_id=1, replica_groups={{0,64,128,192,8,72,136,200},{24,88,152,216,16,80,144,208},{32,96,160,22..., dimensions={0} | all-to-all | bytes 4194304 | tf_op jit(solution)/shard_map/all_to_all | solution.py:251
  120.6 0.2 fusion.2
  120.8 8.2 %collective-permute-start.2 = (f32[128,512]{1,0:T(8,128)S(1)}, f32[128,512]{1,0:T(8,128)S(1)}, u32[]{:S(2)}, u32[]{:S(2)}) collective-permute-start(f32[128,512]{1,0:T(8,128)S(1)} %fusion.2), channel_id=1, source_target_pairs={{0,24},{24,0},{16,40},{40,16},{32,56},{56,32},{48,8},{8,48},{64,88... | collective-permute-start | bytes 786440 | tf_op jit(solution)/shard_map/ppermute | solution.py:257
  129.0 6.7 %collective-permute-done.2 = f32[128,512]{1,0:T(8,128)S(1)} collective-permute-done((f32[128,512]{1,0:T(8,128)S(1)}, f32[128,512]{1,0:T(8,128)S(1)}, u32[]{:S(2)}, u32[]{:S(2)}) %collective-permute-start.2) | collective-permute-done | bytes 262176 | tf_op jit(solution)/shard_map/ppermute | solution.py:257
  135.7 0.3 fusion.13
  136.0 4.2 %collective-permute-start.3 = (f32[128,512]{1,0:T(8,128)S(1)}, f32[128,512]{1,0:T(8,128)S(1)}, u32[]{:S(2)}, u32[]{:S(2)}) collective-permute-start(f32[128,512]{1,0:T(8,128)S(1)} %fusion.13), channel_id=1, source_target_pairs={{8,16},{16,8},{24,32},{32,24},{40,48},{48,40},{56,0},{0,56},{72,80... | collective-permute-start | bytes 786440 | tf_op jit(solution)/shard_map/ppermute | solution.py:257
  140.2 4.4 %collective-permute-done.3 = f32[128,512]{1,0:T(8,128)S(1)} collective-permute-done((f32[128,512]{1,0:T(8,128)S(1)}, f32[128,512]{1,0:T(8,128)S(1)}, u32[]{:S(2)}, u32[]{:S(2)}) %collective-permute-start.3) | collective-permute-done | bytes 262176 | tf_op jit(solution)/shard_map/ppermute | solution.py:257
  144.7 0.2 broadcast_in_dim.7
  144.9 22.7 %all_to_all.45 = bf16[8,2,128,512]{3,2,1,0:T(8,128)(2,1)} all-to-all(bf16[8,2,128,512]{3,2,1,0:T(8,128)(2,1)S(1)} %broadcast_in_dim.7), channel_id=1, replica_groups={{0,64,128,192,8,72,136,200},{24,88,152,216,16,80,144,208},{32,96,160,22..., dimensions={0} | all-to-all | bytes 4194304 | tf_op jit(solution)/shard_map/all_to_all | solution.py:261
  167.6 10.7 %shard_map.43 = bf16[4,256,512]{2,1,0:T(8,128)(2,1)S(1)} custom-call(bf16[4,2,2,128,512]{4,3,2,1,0:T(8,128)(2,1)} %bitcast.33, bf16[1024,2048]{1,0:T(8,128)(2,1)} %keys_hbm.7), custom_call_target="tpu_custom_call" | custom-call | tf_op jit(solution)/shard_map/pallas_call | solution.py:228
  178.4 16.7 %all_to_all.46 = bf16[8,128,512]{2,1,0:T(8,128)(2,1)S(1)} all-to-all(bf16[8,128,512]{2,1,0:T(8,128)(2,1)S(1)} %bitcast.32), channel_id=1, replica_groups={{0,64,128,192,8,72,136,200},{24,88,152,216,16,80,144,208},{32,96,160,22..., dimensions={0} | all-to-all | bytes 2097152 | tf_op jit(solution)/shard_map/all_to_all | solution.py:251
  195.2 1.9 collective-permute-start.4
  197.2 7.3 %collective-permute-done.4 = bf16[128,512]{1,0:T(8,128)(2,1)S(1)} collective-permute-done((bf16[128,512]{1,0:T(8,128)(2,1)S(1)}, bf16[128,512]{1,0:T(8,128)(2,1)S(1)}, u32[]{:S(2)}, u32[]{:S(2)}) %collective-permute-start.4) | collective-permute-done | bytes 131104 | tf_op jit(solution)/shard_map/ppermute | solution.py:257
  204.7 2.2 collective-permute-start.5
  206.9 2.9 %collective-permute-done.5 = bf16[128,512]{1,0:T(8,128)(2,1)S(1)} collective-permute-done((bf16[128,512]{1,0:T(8,128)(2,1)S(1)}, bf16[128,512]{1,0:T(8,128)(2,1)S(1)}, u32[]{:S(2)}, u32[]{:S(2)}) %collective-permute-start.5) | collective-permute-done | bytes 131104 | tf_op jit(solution)/shard_map/ppermute | solution.py:257
  210.0 13.4 %all_to_all.47 = bf16[8,1,128,512]{3,2,1,0:T(8,128)(2,1)S(1)} all-to-all(bf16[8,1,128,512]{3,2,1,0:T(8,128)(2,1)S(1)} %broadcast_in_dim.8), channel_id=1, replica_groups={{0,64,128,192,8,72,136,200},{24,88,152,216,16,80,144,208},{32,96,160,22..., dimensions={0} | all-to-all | bytes 2097152 | tf_op jit(solution)/shard_map/all_to_all | solution.py:261
  223.3 8.2 %shard_map.44 = (f32[256,256]{1,0:T(8,128)S(1)}, bf16[1024,256]{1,0:T(8,128)(2,1)}) custom-call(bf16[4,256,512]{2,1,0:T(8,128)(2,1)S(1)} %bitcast.28, bf16[1024,2048]{1,0:T(8,128)(2,1)} %keys_hbm.7), custom_call_target="tpu_custom_call" | custom-call | tf_op jit(solution)/shard_map/pallas_call | solution.py:228
  231.6 7.0 %all-to-all-start.6 = ((bf16[32,32,256]{2,1,0:T(8,128)(2,1)}), bf16[32,32,256]{2,1,0:T(8,128)(2,1)S(1)}, u32[]{:S(2)}, u32[]{:S(2)}) async-start(bf16[32,32,256]{2,1,0:T(8,128)(2,1)} %bitcast.13), calls=%async_computation.6 | async-start | bytes 1048576 | tf_op jit(solution)/shard_map/all_to_all | solution.py:285
  238.6 2.2 shard_map.45
  240.8 11.3 %all-to-all-done.6 = bf16[32,32,256]{2,1,0:T(8,128)(2,1)S(1)} async-done(((bf16[32,32,256]{2,1,0:T(8,128)(2,1)}), bf16[32,32,256]{2,1,0:T(8,128)(2,1)S(1)}, u32[]{:S(2)}, u32[]{:S(2)}) %all-to-all-start.6) | async-done | bytes 524320 | tf_op jit(solution)/shard_map/all_to_all | solution.py:285
  252.1 0.8 copy.5
  (8 shorter events, 0.6 us)
Async XLA Ops:
  36.9 12.6 %collective-permute-start = (f32[128,512]{1,0:T(8,128)S(1)}, f32[128,512]{1,0:T(8,128)S(1)}, u32[]{:S(2)}, u32[]{:S(2)}) collective-permute-start(f32[128,512]{1,0:T(8,128)S(1)} %fusion.6), channel_id=1, source_target_pairs={{0,24},{24,0},{16,40},{40,16},{32,56},{56,32},{48,8},{8,48},{64,88... | collective-permute-start | bytes 786440 | tf_op jit(solution)/shard_map/ppermute | solution.py:257
  49.8 6.5 %collective-permute-start.1 = (f32[128,512]{1,0:T(8,128)S(1)}, f32[128,512]{1,0:T(8,128)S(1)}, u32[]{:S(2)}, u32[]{:S(2)}) collective-permute-start(f32[128,512]{1,0:T(8,128)S(1)} %fusion.14), channel_id=1, source_target_pairs={{8,16},{16,8},{24,32},{32,24},{40,48},{48,40},{56,0},{0,56},{72,80... | collective-permute-start | bytes 786440 | tf_op jit(solution)/shard_map/ppermute | solution.py:257
  120.8 14.9 %collective-permute-start.2 = (f32[128,512]{1,0:T(8,128)S(1)}, f32[128,512]{1,0:T(8,128)S(1)}, u32[]{:S(2)}, u32[]{:S(2)}) collective-permute-start(f32[128,512]{1,0:T(8,128)S(1)} %fusion.2), channel_id=1, source_target_pairs={{0,24},{24,0},{16,40},{40,16},{32,56},{56,32},{48,8},{8,48},{64,88... | collective-permute-start | bytes 786440 | tf_op jit(solution)/shard_map/ppermute | solution.py:257
  136.0 8.6 %collective-permute-start.3 = (f32[128,512]{1,0:T(8,128)S(1)}, f32[128,512]{1,0:T(8,128)S(1)}, u32[]{:S(2)}, u32[]{:S(2)}) collective-permute-start(f32[128,512]{1,0:T(8,128)S(1)} %fusion.13), channel_id=1, source_target_pairs={{8,16},{16,8},{24,32},{32,24},{40,48},{48,40},{56,0},{0,56},{72,80... | collective-permute-start | bytes 786440 | tf_op jit(solution)/shard_map/ppermute | solution.py:257
  195.2 9.3 %collective-permute-start.4 = (bf16[128,512]{1,0:T(8,128)(2,1)S(1)}, bf16[128,512]{1,0:T(8,128)(2,1)S(1)}, u32[]{:S(2)}, u32[]{:S(2)}) collective-permute-start(bf16[128,512]{1,0:T(8,128)(2,1)S(1)} %fusion.10), channel_id=1, source_target_pairs={{0,24},{24,0},{16,40},{40,16},{32,56},{56,32},{48,8},{8,48},{64,88... | collective-permute-start | bytes 393224 | tf_op jit(solution)/shard_map/ppermute | solution.py:257
  204.7 5.2 %collective-permute-start.5 = (bf16[128,512]{1,0:T(8,128)(2,1)S(1)}, bf16[128,512]{1,0:T(8,128)(2,1)S(1)}, u32[]{:S(2)}, u32[]{:S(2)}) collective-permute-start(bf16[128,512]{1,0:T(8,128)(2,1)S(1)} %add_convert_fusion.1), channel_id=1, source_target_pairs={{8,16},{16,8},{24,32},{32,24},{40,48},{48,40},{56,0},{0,56},{72,80... | collective-permute-start | bytes 393224 | tf_op jit(solution)/shard_map/ppermute | solution.py:257
  231.6 20.5 %all-to-all-start.6 = ((bf16[32,32,256]{2,1,0:T(8,128)(2,1)}), bf16[32,32,256]{2,1,0:T(8,128)(2,1)S(1)}, u32[]{:S(2)}, u32[]{:S(2)}) async-start(bf16[32,32,256]{2,1,0:T(8,128)(2,1)} %bitcast.13), calls=%async_computation.6 | async-start | bytes 1048576 | tf_op jit(solution)/shard_map/all_to_all | solution.py:285
